TPU v7x, 32 devices: a whole 2x2x4 slice. The times are simulated.
32 devices in a mesh: dp: 4 (over y, x), tensor: 8 (over z, core).
Axes of the slice: x: 2, y: 2, z: 4, core: 2. Of those that a mesh axis runs over, the one named last changes fastest.
Arguments:
- inputs: bfloat16 [3072, 4096], P('dp', 'tensor'), may hold values from -6 to 6
- cotangent: bfloat16 [3072, 4096], P('dp', 'tensor'), may hold values from -0.059814453 to 0.059814453
- gate_pre: bfloat16 [3072, 18432], P('dp', 'tensor'), may hold values from -6 to 6
- up_pre: bfloat16 [3072, 18432], P('dp', 'tensor'), may hold values from -6 to 6
- down_weight: bfloat16 [18432, 4096], P('tensor'), may hold values from -0.046875 to 0.046875
- gate_a: bfloat16 [4096, 64], P('tensor'), may hold values from -0.09375 to 0.09375
- gate_b: bfloat16 [64, 18432], P(None, 'tensor'), may hold values from -0.75 to 0.75
- up_a: bfloat16 [4096, 64], P('tensor'), may hold values from -0.09375 to 0.09375
- up_b: bfloat16 [64, 18432], P(None, 'tensor'), may hold values from -0.75 to 0.75
- down_a: bfloat16 [18432, 64], P('tensor'), may hold values from -0.046875 to 0.046875
- down_adapter_second: bfloat16 [64, 4096], P(None, 'tensor'), may hold values from -0.75 to 0.75
Outputs:
- gate_first_gradient: float32 [4096, 64], P('tensor')
- gate_second_gradient: float32 [64, 18432], P(None, 'tensor')
- up_first_gradient: float32 [4096, 64], P('tensor')
- up_second_gradient: float32 [64, 18432], P(None, 'tensor')
- grad_down_a: float32 [18432, 64], P('tensor')
- down_second_gradient: float32 [64, 4096], P(None, 'tensor')
All inputs are finite; a program needn't handle non-finite values.
Results may differ from a plain program's by a relative error of at most 0.005.
Values may be sent and summed in bfloat16 or wider, within the bound.
No kernel may reach another device: no remote copies, remote signals or barrier semaphores. Data moves between devices by JAX's collectives and lax.ppermute only.
A program may use at most 128 MiB of HBM per device.

v0:
```python
import jax
import jax.numpy as jnp
from jax import lax
from jax.sharding import PartitionSpec as P

adapter_scale_factor = 2.0


def silu_parts(pre):
    sigma = jax.nn.sigmoid(pre)
    return (pre * sigma, sigma * (1.0 + pre * (1.0 - sigma)))


def matrix_multiply(left, right):
    return jnp.dot(left, right, preferred_element_type=jnp.float32)


def contract_last(left, right):
    return lax.dot_general(
        left, right, (((1,), (1,)), ((), ())), preferred_element_type=jnp.float32
    )


def contract_leading_axis(left, right):
    return lax.dot_general(
        left, right, (((0,), (0,)), ((), ())), preferred_element_type=jnp.float32
    )


def local(
    inputs,
    cotangent,
    gate_pre,
    up_pre,
    down_weight,
    gate_a,
    gate_b,
    up_a,
    up_b,
    down_a,
    down_adapter_second,
):
    gate_wide = gate_pre.astype(jnp.float32)
    up_wide = up_pre.astype(jnp.float32)
    active, slope = silu_parts(gate_wide)
    hidden = (active * up_wide).astype(jnp.bfloat16)
    gate_part = matrix_multiply(inputs, gate_a)
    up_part = matrix_multiply(inputs, up_a)
    down_part = matrix_multiply(hidden, down_a)
    back_part = contract_last(cotangent, down_adapter_second)
    gate_sum, up_sum, down_sum, backward_total_sum = lax.psum(
        (gate_part, up_part, down_part, back_part), "tensor"
    )
    hidden_base = contract_last(
        lax.all_gather(cotangent, "tensor", axis=1, tiled=True), down_weight
    )
    gate_reduced_rank = gate_sum.astype(jnp.bfloat16)
    up_reduced_rank = up_sum.astype(jnp.bfloat16)
    down_reduced_rank = down_sum.astype(jnp.bfloat16)
    down_backward = (adapter_scale_factor * backward_total_sum).astype(jnp.bfloat16)
    hidden_grad = hidden_base + contract_last(down_backward, down_a)
    grad_down_a = contract_leading_axis(hidden, down_backward)
    down_second_gradient = adapter_scale_factor * contract_leading_axis(
        down_reduced_rank, cotangent
    )
    gate_gradient = (hidden_grad * up_wide * slope).astype(jnp.bfloat16)
    up_gradient = (hidden_grad * active).astype(jnp.bfloat16)
    gate_total, up_total = lax.psum(
        (contract_last(gate_gradient, gate_b), contract_last(up_gradient, up_b)), "tensor"
    )
    gate_backward = gate_total.astype(jnp.bfloat16)
    up_backward = up_total.astype(jnp.bfloat16)
    gate_second_gradient = adapter_scale_factor * contract_leading_axis(
        gate_reduced_rank, gate_gradient
    )
    up_second_gradient = adapter_scale_factor * contract_leading_axis(up_reduced_rank, up_gradient)
    gate_first_gradient = adapter_scale_factor * contract_leading_axis(inputs, gate_backward)
    up_first_gradient = adapter_scale_factor * contract_leading_axis(inputs, up_backward)
    (
        gate_first_gradient,
        gate_second_gradient,
        up_first_gradient,
        up_second_gradient,
        grad_down_a,
        down_second_gradient,
    ) = lax.psum(
        (
            gate_first_gradient,
            gate_second_gradient,
            up_first_gradient,
            up_second_gradient,
            grad_down_a,
            down_second_gradient,
        ),
        "dp",
    )
    return (
        gate_first_gradient,
        gate_second_gradient,
        up_first_gradient,
        up_second_gradient,
        grad_down_a,
        down_second_gradient,
    )


def solution(mesh):
    placed = (
        P("dp", "tensor"),
        P("dp", "tensor"),
        P("dp", "tensor"),
        P("dp", "tensor"),
        P("tensor", None),
        P("tensor", None),
        P(None, "tensor"),
        P("tensor", None),
        P(None, "tensor"),
        P("tensor", None),
        P(None, "tensor"),
    )
    return jax.shard_map(
        local,
        mesh=mesh,
        in_specs=placed,
        out_specs=(
            P("tensor", None),
            P(None, "tensor"),
            P("tensor", None),
            P(None, "tensor"),
            P("tensor", None),
            P(None, "tensor"),
        ),
        check_vma=False,
    )
```

profile of v0, /device:TPU:0, one launch (start us, length us, event | category | flops | bytes accessed | tf_op | source)
XLA Modules:
  0.0 333.2 jit_solution(9101113223942023425)
XLA Ops:
  7.2 0.0 copy-start
  7.2 0.0 all-reduce.6.cloned.1.call-start
  7.2 2.2 fusion.19
  9.5 0.0 all-reduce.6.cloned.1.call-update
  9.5 0.0 all-gather.2.cloned.1.call-start
  9.5 0.7 all-gather.2.cloned.1.call-update
  10.2 0.0 all-reduce.8.cloned.1.call-start
  10.3 1.2 fusion.21
  11.5 1.2 fusion.23
  12.7 55.5 %all-reduce.6.cloned.1.call-done = f32[768,64]{0,1:T(8,128)} async-done(((f32[768,64]{0,1:T(8,128)}), f32[768,64]{0,1:T(8,128)}) %all-reduce.6.cloned.1.call-update) | async-done | bytes 196624 | tf_op jit(solution)/shard_map/psum | solution.py:51
  68.2 5.1 %fusion.16 = f32[768,2304]{1,0:T(8,128)} fusion(bf16[2304,64]{0,1:T(8,128)(2,1)} %param.20, f32[768,64]{0,1:T(8,128)} %all-reduce.6.cloned.1.call-done), kind=kOutput, calls=%fused_computation.29 | convolution fusion | flops 226590720 | bytes 7569408 | tf_op jit(solution)/shard_map/dot_general | solution.py:19
  73.3 60.3 %all-gather.2.cloned.1.call-done = bf16[768,4096]{1,0:T(8,128)(2,1)} async-done(((bf16[768,512]{1,0:T(8,128)(2,1)}), bf16[768,4096]{1,0:T(8,128)(2,1)}) %all-gather.2.cloned.1.call-update) | async-done | bytes 6291472 | tf_op jit(solution)/shard_map/all_gather | solution.py:55
  133.7 25.8 %multiply_convert_fusion = (bf16[768,2304]{1,0:T(8,128)(2,1)}, bf16[768,2304]{1,0:T(8,128)(2,1)}, bf16[768,2304]{1,0:T(8,128)(2,1)S(1)}) fusion(bf16[768,2304]{1,0:T(8,128)(2,1)} %param.13, bf16[768,2304]{1,0:T(8,128)(2,1)} %param.14, f32[768,2304]{1,0:T(8,128)} %fusion.16, bf16[768,4096]{1,0:T(8,128)(2,1)} %all-gather.2.cloned.1.call-done, ...), kind=kOutput, calls=%fused_computation.13 | convolution fusion | flops 14527365120 | bytes 49938432 | tf_op jit(solution)/shard_map/dot_general | solution.py:19
  159.5 5.1 %fusion.20 = f32[768,64]{1,0:T(8,128)} fusion(bf16[768,2304]{1,0:T(8,128)(2,1)} %get-tuple-element.18, bf16[64,2304]{1,0:T(8,128)(2,1)} %param.17), kind=kOutput, calls=%fused_computation.33 | convolution fusion | flops 226492416 | bytes 4030464 | tf_op jit(solution)/shard_map/dot_general | solution.py:19
  164.6 3.8 %fusion.22 = f32[768,64]{1,0:T(8,128)} fusion(bf16[768,2304]{1,0:T(8,128)(2,1)} %get-tuple-element.17, bf16[64,2304]{1,0:T(8,128)(2,1)} %param.19), kind=kOutput, calls=%fused_computation.35 | convolution fusion | flops 226492416 | bytes 4030464 | tf_op jit(solution)/shard_map/dot_general | solution.py:19
  168.4 0.0 copy-done.2
  168.5 1.8 fusion.24
  170.3 62.1 %all-reduce.9 = (bf16[768,64]{1,0:T(8,128)(2,1)S(1)}, bf16[768,64]{1,0:T(8,128)(2,1)S(1)}, bf16[768,64]{1,0:T(8,128)(2,1)S(1)}, bf16[768,64]{1,0:T(8,128)(2,1)S(1)}, bf16[768,64]{1,0:T(8,128)(2,1)S(1)}) all-reduce(f32[768,64]{1,0:T(8,128)} %fusion.20, f32[768,64]{1,0:T(8,128)S(1)} %fusion.21, ...), channel_id=1, replica_groups=mesh['dp'=4,'tensor'=8] {'tensor'}, use_global_device_ids=true, to_apply=%region_1.0 | all-reduce | flops 245760 | bytes 1474560 | tf_op jit(solution)/shard_map/psum | solution.py:68
  232.4 3.7 %convolution_multiply_fusion = f32[64,2304]{1,0:T(8,128)} fusion(bf16[768,2304]{1,0:T(8,128)(2,1)} %get-tuple-element.17, bf16[768,64]{1,0:T(8,128)(2,1)S(1)} %get-tuple-element.9), kind=kOutput, calls=%fused_computation.15 | convolution fusion | flops 226639872 | bytes 4227072 | tf_op jit(solution)/shard_map/dot_general | solution.py:25
  236.1 3.6 %convolution_multiply_fusion.1 = f32[64,2304]{1,0:T(8,128)} fusion(bf16[768,2304]{1,0:T(8,128)(2,1)} %get-tuple-element.18, bf16[768,64]{1,0:T(8,128)(2,1)S(1)} %get-tuple-element.7), kind=kOutput, calls=%fused_computation.16 | convolution fusion | flops 226639872 | bytes 4227072 | tf_op jit(solution)/shard_map/dot_general | solution.py:25
  239.7 0.9 convolution_multiply_fusion.2
  240.6 0.9 fusion.8
  241.6 0.9 fusion.9
  242.5 1.6 fusion.15
  244.1 0.0 all-reduce.8.cloned.1.call-update
  244.1 72.1 %all-reduce.8.cloned.1.call-done = (f32[512,64]{0,1:T(8,128)}, f32[64,2304]{1,0:T(8,128)}, f32[512,64]{0,1:T(8,128)}, f32[64,2304]{1,0:T(8,128)}, f32[2304,64]{0,1:T(8,128)}, /*index=5*/f32[64,512]{1,0:T(8,128)}) async-done(((f32[512,64]{0,1:T(8,128)}, f32[64,2304]{1,0:T(8,128)}, f32[512,64]{0,1:T(8,128)}, f32[64,2304]{1,0:T(8,128)}, f32[2304,64]{0,1:T(8,128)}, /*index=5*/f32[64,512]{1,0:T(8,128)}), ...) | async-done | bytes 2162704 | tf_op jit(solution)/shard_map/psum | solution.py:86
  316.2 1.6 copy.34
  317.7 1.9 copy.35
  319.7 1.6 copy.36
  321.2 1.9 copy.37
  323.1 1.9 copy.38
  325.1 1.6 copy.39
  (10 shorter events, 0.0 us)
Async XLA Ops:
  7.2 3.1 copy-start
  7.2 61.0 %all-reduce.6.cloned.1.call-start = ((), (), s32[]{:S(2)}) async-start(), calls=%async_computation.1 | async-start | bytes 393216 | tf_op jit(solution)/shard_map/psum | solution.py:51
  9.5 124.2 %all-gather.2.cloned.1.call-start = ((), (), s32[]{:S(2)}) async-start(), calls=%async_computation | async-start | bytes 7077888 | tf_op jit(solution)/shard_map/all_gather | solution.py:55
  10.2 305.9 %all-reduce.8.cloned.1.call-start = ((), (), s32[]{:S(2)}) async-start(), calls=%async_computation.2 | async-start | bytes 4325376 | tf_op jit(solution)/shard_map/psum | solution.py:86
  159.5 9.0 %copy-start.2 = (bf16[768,2304]{1,0:T(8,128)(2,1)}, bf16[768,2304]{1,0:T(8,128)(2,1)S(1)}, u32[]{:S(2)}) copy-start(bf16[768,2304]{1,0:T(8,128)(2,1)S(1)} %get-tuple-element.19) | copy-start | bytes 10616836
  159.5 9.0 %copy-start.5 = (bf16[2304,64]{0,1:T(8,128)(2,1)S(1)}, bf16[2304,64]{0,1:T(8,128)(2,1)}, u32[]{:S(2)}) copy-start(bf16[2304,64]{0,1:T(8,128)(2,1)} %param.20) | copy-start | bytes 884740
  170.3 69.4 %copy-start.1 = (bf16[768,512]{1,0:T(8,128)(2,1)S(1)}, bf16[768,512]{1,0:T(8,128)(2,1)}, u32[]{:S(2)}) copy-start(bf16[768,512]{1,0:T(8,128)(2,1)} %param.12) | copy-start | bytes 2359300
  232.3 10.2 %copy-start.3 = (bf16[768,2304]{1,0:T(8,128)(2,1)S(1)}, bf16[768,2304]{1,0:T(8,128)(2,1)}, u32[]{:S(2)}) copy-start(bf16[768,2304]{1,0:T(8,128)(2,1)} %copy-done.2) | copy-start | bytes 10616836
  232.3 10.2 %copy-start.4 = (f32[768,64]{0,1:T(8,128)S(1)}, f32[768,64]{0,1:T(8,128)}, u32[]{:S(2)}) copy-start(f32[768,64]{0,1:T(8,128)} %all-reduce.6.cloned.1.call-done) | copy-start | bytes 589828
Sparse Core Ops, SparseCore 0:
  10.9 57.2 all-reduce.5
  69.9 63.6 all-gather.1
  244.2 71.9 all-reduce.7
where the time goes:
time: 334 us; the launch traced here: 333 us
  waiting for transfers between devices  189 us (57%)
  blocking collectives  62.1 us (19%)
  matrix products  58 us (17%)
  between operations  13.8 us (4%)
  local copies, waits for them, and re-layouts  10.5 us (3%)
    psum x1, waiting for transfers between devices, local(): lax.psum((gate_first_gradient, gate_second_gradient, up_first_gradient, u...  72.1 us
    psum x1, blocking collectives, local(): lax.psum((contract_last(gate_gradient, gate_b), contract_last(up_gradient...  62.1 us
    all_gather x1, waiting for transfers between devices, local(): lax.all_gather(cotangent, 'tensor', axis=1, tiled=True)  60.3 us
    psum x1, waiting for transfers between devices, local(): lax.psum((gate_part, up_part, down_part, back_part), 'tensor')  55.5 us
    dot_general x5, matrix products, contract_last(): lax.dot_general(left, right, (((1,), (1,)), ((), ())), preferred_element_...  42.1 us
    dot_general x6, matrix products, contract_leading_axis(): lax.dot_general(left, right, (((0,), (0,)), ((), ())), preferred_element_...  11.7 us
    unnamed x18, local copies, waits for them, and re-layouts  10.5 us
  transfers between devices with their start and end apart: 3, of which 3 were waited for; matrix products, arithmetic and copies ran while one was open for 2% of the time, Pallas kernels for 0%

commit v1 on v0

v1 whole, which is shorter than its diff:
```python
import functools

import jax
import jax.numpy as jnp
from jax import lax
from jax.experimental import pallas as pl
from jax.experimental.pallas import tpu as pltpu
from jax.sharding import PartitionSpec as P

adapter_scale_factor = 2.0
LANES = 128
BF = jnp.bfloat16
F32 = jnp.float32


def silu_parts(pre):
    sigma = 0.5 + 0.5 * jnp.tanh(0.5 * pre)
    return pre * sigma, sigma * (1.0 + pre * (1.0 - sigma))


def dot_nt(left, right):
    return lax.dot_general(left, right, (((1,), (1,)), ((), ())), preferred_element_type=F32)


def dot_nn(left, right):
    return jnp.dot(left, right, preferred_element_type=F32)


def dot_tn(left, right):
    return lax.dot_general(left, right, (((0,), (0,)), ((), ())), preferred_element_type=F32)


def pin(x, *after):
    return lax.optimization_barrier((x, *after))[0]


def divisor(size, most):
    best = LANES
    for width in range(LANES, most + 1, LANES):
        if size % width == 0:
            best = width
    return best


def cost(flops, moved, transcendentals=0):
    return pl.CostEstimate(flops=flops, bytes_accessed=moved, transcendentals=transcendentals)


def grad_kernel(n_blocks, has_acc, finish, first, final, *refs):
    blocks = refs[2 : 2 + n_blocks]
    weights = refs[2 + n_blocks : 2 + 2 * n_blocks]
    refs = refs[2 + 2 * n_blocks :]
    grad = dot_nt(blocks[0][...], weights[0][...])
    for block, w_ref in zip(blocks[1:], weights[1:]):
        grad = grad + dot_nt(block[...], w_ref[...])
    if has_acc:
        grad = grad + refs[0][...]
        refs = refs[1:]
    if not finish:
        refs[0][...] = grad
        return
    back_ref, da_ref, factor_ref, act_ref, gb_ref, ub_ref, low_ref = refs[:7]
    part_ref = refs[-3 if final else -2]
    step = pl.program_id(0)
    grad = grad + dot_tn(back_ref[...], da_ref[...])
    gate_grad = (grad * factor_ref[...]).astype(BF)
    up_grad = (grad * act_ref[...]).astype(BF)
    zeros = jnp.zeros_like(gb_ref)
    part = dot_nt(gate_grad, jnp.concatenate([gb_ref[...], zeros], axis=0))
    part = part + dot_nt(up_grad, jnp.concatenate([zeros, ub_ref[...]], axis=0))

    @pl.when(step == 0)
    def _():
        part_ref[...] = part

    @pl.when(step > 0)
    def _():
        part_ref[...] += part

    rank = low_ref.shape[0] // 2
    gate_second = dot_nn(low_ref[:rank, :], gate_grad)
    up_second = dot_nn(low_ref[rank:, :], up_grad)
    if not first:
        gate_second = refs[7][:rank, :] + gate_second
        up_second = refs[7][rank:, :] + up_second
    if final:
        refs[-2][...] = gate_second.astype(BF)
        refs[-1][...] = up_second.astype(BF)
    else:
        refs[-1][:rank, :] = gate_second
        refs[-1][rank:, :] = up_second


def grad_call(name, span, table, me, pieces, weight, acc, rest=None, second=None, final=False):
    at, size = span
    index = at // size
    hidden = weight.shape[0]
    blocks = [block for _, block in pieces]
    width = blocks[0].shape[1]
    tile = divisor(hidden, 768)
    finish = rest is not None
    per = int(round(table.shape[0] ** 0.5))
    in_specs = [pl.BlockSpec((size, width), lambda j, t, m: (0, 0)) for _ in blocks]
    for column, _ in pieces:
        in_specs.append(
            pl.BlockSpec(
                (tile, width), lambda j, t, m, column=column: (j, t[m[0] * per + column])
            )
        )
    args = [*blocks, *[weight] * len(blocks)]
    if acc is not None:
        in_specs.append(pl.BlockSpec((size, tile), lambda j, t, m: (index, j)))
        args.append(acc)
    flops = 2 * size * hidden * width * len(blocks)
    moved = 2 * hidden * width * len(blocks) + 8 * size * hidden
    if finish:
        back, low = rest[0], rest[-1]
        ranks = low.shape[0]
        rank = ranks // 2
        flops += 2 * size * hidden * 8 * ranks
        in_specs += [
            pl.BlockSpec((rank, size), lambda j, t, m: (0, index)),
            pl.BlockSpec((rank, tile), lambda j, t, m: (0, j)),
            pl.BlockSpec((size, tile), lambda j, t, m: (index, j)),
            pl.BlockSpec((size, tile), lambda j, t, m: (index, j)),
            pl.BlockSpec((rank, tile), lambda j, t, m: (0, j)),
            pl.BlockSpec((rank, tile), lambda j, t, m: (0, j)),
            pl.BlockSpec((ranks, size), lambda j, t, m: (0, index)),
        ]
        args += rest
        if second is not None:
            in_specs.append(pl.BlockSpec((ranks, tile), lambda j, t, m: (0, j)))
            args.append(second)
        out_specs = [pl.BlockSpec((size, ranks), lambda j, t, m: (0, 0))]
        out_shape = [jax.ShapeDtypeStruct((size, ranks), F32)]
        if final:
            out_specs += [pl.BlockSpec((rank, tile), lambda j, t, m: (0, j))] * 2
            out_shape += [jax.ShapeDtypeStruct((rank, hidden), BF)] * 2
        else:
            out_specs.append(pl.BlockSpec((ranks, tile), lambda j, t, m: (0, j)))
            out_shape.append(jax.ShapeDtypeStruct((ranks, hidden), F32))
    else:
        out_specs = pl.BlockSpec((size, tile), lambda j, t, m: (0, j))
        out_shape = jax.ShapeDtypeStruct((size, hidden), F32)
    return pl.pallas_call(
        functools.partial(
            grad_kernel, len(blocks), acc is not None, finish, second is None, final
        ),
        grid_spec=pltpu.PrefetchScalarGridSpec(
            num_scalar_prefetch=2,
            grid=(hidden // tile,),
            in_specs=in_specs,
            out_specs=out_specs,
        ),
        out_shape=out_shape,
        compiler_params=pltpu.CompilerParams(vmem_limit_bytes=36 * 1024 * 1024),
        cost_estimate=cost(flops, moved),
        name=name,
    )(table, me, *args)


def low_kernel(x_ref, ga_ref, ua_ref, cot_ref, s_ref, low_ref):
    rank = s_ref.shape[0]
    both = jnp.concatenate([ga_ref[...], ua_ref[...]], axis=0)
    low_ref[: 2 * rank, :] = dot_nt(x_ref[...], both).T
    back = adapter_scale_factor * dot_nt(cot_ref[...], s_ref[...])
    low_ref[2 * rank :, :] = back.T


def low_call(inputs, ga, ua, cotangent, second):
    return pl.pallas_call(
        low_kernel,
        out_shape=jax.ShapeDtypeStruct((3 * second.shape[0], inputs.shape[0]), F32),
        compiler_params=pltpu.CompilerParams(vmem_limit_bytes=60 * 1024 * 1024),
        cost_estimate=cost(1024, 1024),
        name="low",
    )(inputs, ga, ua, cotangent, second)


def hidden_kernel(gate_ref, up_ref, da_ref, down_ref, hidden_ref, factor_ref, act_ref, acc_ref):
    step = pl.program_id(0)
    up = up_ref[...].astype(F32)
    act, slope = silu_parts(gate_ref[...].astype(F32))
    factor_ref[...] = up * slope
    act_ref[...] = act
    hidden = (act * up).astype(BF)
    hidden_ref[...] = hidden
    part = dot_nt(hidden, da_ref[...])

    @pl.when(step == 0)
    def _():
        acc_ref[...] = part

    @pl.when(step > 0)
    def _():
        acc_ref[...] += part

    @pl.when(step == pl.num_programs(0) - 1)
    def _():
        turned = acc_ref[...].T
        rank = turned.shape[0]
        for i in range(turned.shape[1] // LANES):
            down_ref[i * rank : (i + 1) * rank, :] = turned[:, i * LANES : (i + 1) * LANES]


def hidden_call(gate_pre, up_pre, da):
    tokens, hidden = gate_pre.shape
    rank = da.shape[0]
    tile = divisor(hidden, 384)
    rows = rank * tokens // LANES
    wide = pl.BlockSpec((tokens, tile), lambda j: (0, j))
    return pl.pallas_call(
        hidden_kernel,
        grid=(hidden // tile,),
        in_specs=[wide, wide, pl.BlockSpec((rank, tile), lambda j: (0, j))],
        out_specs=[pl.BlockSpec((rows, LANES), lambda j: (0, 0)), wide, wide, wide],
        out_shape=[
            jax.ShapeDtypeStruct((rows, LANES), F32),
            jax.ShapeDtypeStruct((tokens, hidden), BF),
            jax.ShapeDtypeStruct((tokens, hidden), F32),
            jax.ShapeDtypeStruct((tokens, hidden), F32),
        ],
        scratch_shapes=[pltpu.VMEM((tokens, rank), F32)],
        compiler_params=pltpu.CompilerParams(vmem_limit_bytes=60 * 1024 * 1024),
        cost_estimate=cost(1024, 1024),
        name="hidden",
    )(gate_pre, up_pre, da)


def packed(x, plain):
    upper = lax.reduce_precision(x[plain:], exponent_bits=8, mantissa_bits=7)
    rest = x[plain:] - upper
    return jnp.concatenate([x[:plain], upper, rest], axis=0).astype(BF)


def unpacked(x, plain):
    x = x.astype(F32)
    end = (plain + x.shape[0]) // 2
    return jnp.concatenate([x[:plain], x[plain:end] + x[end:]], axis=0)


def summed(values):
    total = values[0].astype(F32)
    for value in values[1:]:
        total = total + value.astype(F32)
    return total


class Places:
    def __init__(self, tensors, dps):
        self.tensors = tensors
        self.chips = tensors // 2
        self.dps = dps
        self.me = lax.axis_index("tensor")
        self.z = lax.shift_right_logical(self.me, 1)
        self.core = lax.bitwise_and(self.me, 1)
        self.swap_pairs = [(i, i ^ 1) for i in range(tensors)]
        chips = self.chips
        self.moves = []
        for chip in range(chips):
            found = []
            for k in range(1, chips):
                found += [(k, d) for d in (-1, 1) if 0 <= chip + d * k < chips]
            self.moves.append(found)
        table = []
        for device in range(tensors):
            chip, c = divmod(device, 2)
            for k, d in [(0, 0)] + self.moves[chip]:
                owner = chip + d * k
                table += [2 * owner + c, 2 * owner + 1 - c]
        self.table = jnp.array(table, jnp.int32)
        self.scalars = {"even": self.core == 0}
        for chip in range(chips):
            self.scalars["chip%d" % chip] = self.z == chip

    def at(self, chips):
        return functools.reduce(jnp.logical_or, [self.scalars["chip%d" % chip] for chip in chips])

    def sources(self, k, d):
        chips = self.chips
        return [i for i in range(chips) if 0 <= i - d < chips and 0 <= i + d * (k - 1) < chips]

    def flood(self, k, up, down):
        pairs = []
        for d in (1, -1):
            pairs.append([(2 * i + c, 2 * (i - d) + c) for i in self.sources(k, d) for c in range(2)])
        if not set(self.sources(k, 1)) & set(self.sources(k, -1)):
            chosen = jnp.where(self.at(self.sources(k, 1)), up, down)
            both = lax.ppermute(chosen, "tensor", pairs[0] + pairs[1])
            return both, both
        return lax.ppermute(up, "tensor", pairs[0]), lax.ppermute(down, "tensor", pairs[1])

    def piece(self, p, ups, downs):
        chosen = []
        for chip in range(self.chips):
            k, d = self.moves[chip][p - 1]
            block = (ups if d > 0 else downs)[k]
            for entry in chosen:
                if entry[0] is block:
                    entry[1].append(chip)
                    break
            else:
                chosen.append((block, [chip]))
        chosen.sort(key=lambda entry: -len(entry[1]))
        result = chosen[0][0]
        for block, chips in chosen[1:]:
            result = jnp.where(self.at(chips), block, result)
        return result

    def swap(self, x):
        return lax.ppermute(x, "tensor", self.swap_pairs)

    def meet(self, low, high):
        even = self.scalars["even"]
        return jnp.where(even, low, high) + self.swap(jnp.where(even, high, low))

    def order(self, total, other):
        even = self.scalars["even"]
        return jnp.where(even, total, other), jnp.where(even, other, total)

    def part(self, total):
        return self.order(total, self.swap(total))

    def inward(self, i):
        last = self.chips - 1
        pairs = []
        for c in range(2):
            pairs.append((2 * i + c, 2 * (i + 1) + c))
            pairs.append((2 * (last - i) + c, 2 * (last - 1 - i) + c))
        return pairs

    def middle(self):
        left = 2 * (self.chips // 2 - 1)
        pairs = []
        for c in range(2):
            pairs += [(left + c, left + 2 + c), (left + 2 + c, left + c)]
        return pairs

    def low_send(self, step, total, plain):
        inner = self.chips // 2 - 1
        if step < inner:
            mine = packed(total, plain)
            pairs = self.inward(step)
        elif step == inner:
            mine = packed(total, plain)
            pairs = self.middle()
        else:
            mine = total
            pairs = [(to, at) for at, to in self.inward(self.chips - 2 - step)]
        return mine, lax.ppermute(mine, "tensor", pairs)

    def low_take(self, step, total, sent, plain):
        mine, got = sent
        inner = self.chips // 2 - 1
        if step < inner:
            return total + unpacked(got, plain)
        if step == inner:
            return (unpacked(mine, plain) + unpacked(got, plain)).astype(BF)
        i = self.chips - 2 - step
        return jnp.where(self.at([i, self.chips - 1 - i]), got, total)

    def send_across(self, total, k):
        pairs = [(i, i ^ (2 * k)) for i in range(self.tensors)]
        mine = total.astype(BF) if 2 * k == self.chips else total
        return mine, lax.ppermute(mine, "tensor", pairs)

    def dp_bits(self, flip):
        bits = [1 << b for b in range(self.dps.bit_length() - 1)]
        return bits[::-1] if flip else bits

    def dp_send(self, part, bit):
        mine = part.astype(BF)
        return mine, lax.ppermute(mine, "dp", [(i, i ^ bit) for i in range(self.dps)])

    def sum_four(self, part, one, other):
        mine = part.astype(BF)
        gots = []
        for bits in (one ^ other, one, other):
            pairs = [(i, i ^ bits) for i in range(self.dps)]
            gots.append(lax.ppermute(mine, "dp", pairs))
        far, near, side = gots
        return summed([mine, near]) + summed([side, far])


def local(
    tensors,
    dps,
    inputs,
    cotangent,
    gate_pre,
    up_pre,
    down_weight,
    gate_a,
    gate_b,
    up_a,
    up_b,
    down_a,
    down_adapter_second,
):
    places = Places(tensors, dps)
    tokens, width = inputs.shape
    rank = gate_b.shape[0]
    hops = places.chips - 1
    barrier = lax.optimization_barrier

    cut = tokens - tokens // 3
    span_a, span_b = (cut, tokens - cut), (0, cut)
    da = down_a.T
    inputs, me, places.scalars = barrier((inputs, places.me.reshape(1), places.scalars))

    def arrived(hop, block):
        return [(2 * hop + 2, block), (2 * hop + 3, places.swap(block))]

    plain = 2 * rank
    up, down = places.flood(1, cotangent, cotangent)
    low_part = low_call(inputs, gate_a.T, up_a.T, cotangent, down_adapter_second)
    swapped = places.swap(cotangent)
    half = low_part.shape[1] // 2
    low_sum = places.meet(low_part[:, :half], low_part[:, half:])
    down_part, hidden, factor, act = hidden_call(gate_pre, up_pre, da)
    up, down, low_sum, down_part = barrier((up, down, low_sum, down_part))
    ups, downs = [None, up], [None, down]

    def rows_of(blocks, span):
        return [block if block is None else block[span[0] : span[0] + span[1]] for block in blocks]

    sent = places.low_send(0, low_sum, plain)
    pieces = [(0, cotangent), (1, swapped)]
    acc = None
    for hop in range(1, hops):
        last = hop == hops - 1
        if last:
            up, down = places.flood(hop + 1, *(rows_of([x[hop]], span_a)[0] for x in (ups, downs)))
        else:
            up, down = places.flood(hop + 1, ups[hop], downs[hop])
        low_sum = places.low_take(hop - 1, low_sum, sent, plain)
        sent = places.low_send(hop, low_sum, plain)
        acc = grad_call(
            "more", (0, tokens), places.table, me,
            pieces + arrived(hop - 1, places.piece(hop, ups, downs)), down_weight, acc,
        )
        pieces = []
        blocks = [up] if up is down else [up, down]
        if last:
            behind = rows_of(ups, span_b), rows_of(downs, span_b)
            blocks, acc, behind = barrier((blocks, acc, behind))
            acc, sent = barrier((acc, sent))
        else:
            blocks, acc = barrier((blocks, acc))
            acc, sent = barrier((acc, sent))
        up, down = blocks[0], blocks[-1]
        if not last:
            ups.append(up)
            downs.append(down)
    low_sum = places.low_take(hops - 1, low_sum, sent, plain)

    held = places.piece(hops, rows_of(ups, span_a) + [up], rows_of(downs, span_a) + [down])
    ups, downs = behind
    up, _ = places.flood(hops, ups[-1], downs[-1])
    low_all = jnp.concatenate(places.part(low_sum), axis=1)
    low = low_all[: 2 * rank] * BF(adapter_scale_factor)
    back = low_all[2 * rank :]
    rest = [back, da, factor, act, gate_b, up_b, low]
    early = places.dp_send(dot_nn(back, hidden), places.dp_bits(False)[0])
    part_a, second = grad_call(
        "last_a", span_a, places.table, me, arrived(hops - 1, held), down_weight, acc, rest
    )
    up, second, part_a, early = barrier((up, second, part_a, early))
    coming = places.piece(hops, ups + [up], downs + [up])
    rows = down_part.shape[0]
    before = places.meet(
        jnp.concatenate([down_part[: rows // 2], part_a[: span_a[1] // 2]], axis=0),
        jnp.concatenate([down_part[rows // 2 :], part_a[span_a[1] // 2 :]], axis=0),
    )
    before = places.send_across(before, 1)
    early = places.dp_send(summed(early), places.dp_bits(False)[1])
    part_b, *large = grad_call(
        "last_b", span_b, places.table, me, arrived(hops - 1, coming), down_weight, acc,
        rest, second, True,
    )
    part_b, before, early = barrier((part_b, before, early))

    bits = [places.dp_bits(flip) for flip in (False, True)]
    sent = [places.dp_send(x, order[0]) for x, order in zip(large, bits)]
    half = part_b.shape[0] // 2
    after = places.meet(part_b[:half], part_b[half:])
    across = places.send_across(after, 1)
    before = summed(before)
    k = 2
    while k < places.chips:
        beside = places.send_across(before, k)
        sent, across = barrier((sent, across))
        if k == 2:
            large = [summed(pair) for pair in sent]
            sent = [places.dp_send(x, order[1]) for x, order in zip(large, bits)]
        across = places.send_across(summed(across), k)
        beside, across = barrier((beside, across))
        before = summed(beside)
        k *= 2
    total = jnp.concatenate([before, summed(across)], axis=0).astype(BF)
    other, sent = barrier((places.swap(total), sent))
    large = [summed(pair) for pair in sent]
    sums = places.order(total, other)
    down_low = jnp.concatenate([both[: rows // 2] for both in sums], axis=0)
    down_low = jnp.concatenate(
        [down_low[i * rank : (i + 1) * rank] for i in range(tokens // LANES)], axis=1
    )
    ends = (rows // 2, rows // 2 + span_a[1] // 2)
    totals = jnp.concatenate(
        [both[ends[1] :] for both in sums] + [both[ends[0] : ends[1]] for both in sums], axis=0
    )
    firsts = jnp.concatenate([dot_tn(totals, inputs), dot_nn(down_low, cotangent)], axis=0)
    firsts = firsts * adapter_scale_factor
    grad_down_t = summed(early)
    for bit in places.dp_bits(False)[2:]:
        grad_down_t = summed(places.dp_send(grad_down_t, bit))
    for i in range(2, len(bits[0])):
        large = [summed(places.dp_send(x, order[i])) for x, order in zip(large, bits)]
    for i in range(0, len(bits[0]), 2):
        firsts = places.sum_four(firsts, bits[0][i], bits[0][i + 1])
    gate_second, up_second = large
    gate_first = firsts[:rank]
    up_first = firsts[rank : 2 * rank]
    down_second = firsts[2 * rank :]
    return (gate_first.T, gate_second, up_first.T, up_second, grad_down_t.T, down_second)


def solution(mesh):
    placed = (
        P("dp", "tensor"),
        P("dp", "tensor"),
        P("dp", "tensor"),
        P("dp", "tensor"),
        P("tensor", None),
        P("tensor", None),
        P(None, "tensor"),
        P("tensor", None),
        P(None, "tensor"),
        P("tensor", None),
        P(None, "tensor"),
    )
    return jax.shard_map(
        functools.partial(local, mesh.shape["tensor"], mesh.shape["dp"]),
        mesh=mesh,
        in_specs=placed,
        out_specs=(
            P("tensor", None),
            P(None, "tensor"),
            P("tensor", None),
            P(None, "tensor"),
            P("tensor", None),
            P(None, "tensor"),
        ),
        check_vma=False,
    )
```

time: 334 us -> 130 us (0.39)
  waiting for transfers between devices: 189 us -> 29.7 us
  blocking collectives: 62.1 us -> 0 us
  matrix products: 58 us -> 1.27 us
  Pallas kernels: 0 us -> 50.8 us
  starting transfers between devices: 0.12 us -> 40.1 us
  between operations: 13.8 us -> 1.38 us
  local copies, waits for them, and re-layouts: 10.5 us -> 1.06 us
  other arithmetic: 0 us -> 5.15 us
    psum x2 -> x0, waiting for transfers between devices: 128 us -> none  [the longest x1 72.1 us: local(): lax.psum((gate_first_gradient, gate_second_gradient, up_first_gradient, u...]
    psum x1 -> x0, blocking collectives: 62.1 us -> none  [local(): lax.psum((contract_last(gate_gradient, gate_b), contract_last(up_gradient...]
    all_gather x1 -> x0, waiting for transfers between devices: 60.3 us -> none  [local(): lax.all_gather(cotangent, 'tensor', axis=1, tiled=True)]
    dot_general x14 -> x3, matrix products: 58 us -> 1.27 us  [the longest x2 0.98 us: dot_nn(): return jnp.dot(left, right, preferred_element_type=F32)]
    pallas_call x0 -> x6, Pallas kernels: none -> 50.8 us  [the longest x4 36.5 us: grad_call(): pl.pallas_call(functools.partial(grad_kernel, len(blocks), acc is not Non...]
    ppermute x0 -> x32, starting transfers between devices: none -> 40.1 us  [the longest x4 7.93 us: send_across(): return (mine, lax.ppermute(mine, 'tensor', pairs))]
    ppermute x0 -> x32, waiting for transfers between devices: none -> 29.7 us  [the longest x2 9.16 us: flood(): both = lax.ppermute(chosen, 'tensor', pairs[0] + pairs[1])]
    unnamed x18 -> x27, local copies, waits for them, and re-layouts: 10.5 us -> 0.1 us
  transfers between devices with their start and end apart: 3 -> 32, of which waited for: 3 -> 14; matrix products, arithmetic and copies ran while one was open for 2% -> 4% of each run, Pallas kernels for 0% -> 39%
where the time goes in v1:
time: 130 us; the launch traced here: 129 us
  Pallas kernels  50.8 us (39%)
  starting transfers between devices  40.1 us (31%)
  waiting for transfers between devices  29.7 us (23%)
  other arithmetic  5.15 us (4%)
  between operations  1.38 us (1%)
    pallas_call x4, Pallas kernels, grad_call(): pl.pallas_call(functools.partial(grad_kernel, len(blocks), acc is not Non...  36.5 us
    pallas_call x1, Pallas kernels, hidden_call(): pl.pallas_call(hidden_kernel, grid=(hidden // tile,), in_specs=[wide, wid...  11.4 us
    ppermute x2, waiting for transfers between devices, flood(): both = lax.ppermute(chosen, 'tensor', pairs[0] + pairs[1])  9.16 us
    ppermute x4, starting transfers between devices, send_across(): return (mine, lax.ppermute(mine, 'tensor', pairs))  7.93 us
    ppermute x2, starting transfers between devices, flood(): lax.ppermute(down, 'tensor', pairs[1])  7.16 us
    ppermute x6, starting transfers between devices, dp_send(): lax.ppermute(mine, 'dp', [(i, i ^ bit) for i in range(self.dps)])  6.98 us
    ppermute x3, starting transfers between devices, low_send(): return (mine, lax.ppermute(mine, 'tensor', pairs))  6.49 us
    ppermute x4, waiting for transfers between devices, send_across(): return (mine, lax.ppermute(mine, 'tensor', pairs))  4.95 us
  transfers between devices with their start and end apart: 32, of which 14 were waited for; matrix products, arithmetic and copies ran while one was open for 4% of the time, Pallas kernels for 39%

profile of v1, /device:TPU:0, one launch (start us, length us, event | category | flops | bytes accessed | tf_op | source)
XLA Modules:
  0.0 129.5 jit_solution(18359510607962914560)
XLA Ops:
  0.6 1.3 collective-permute-start
  1.9 6.4 %collective-permute-start.1 = (bf16[768,512]{1,0:T(8,128)(2,1)}, bf16[768,512]{1,0:T(8,128)(2,1)}, u32[]{:S(2)}, u32[]{:S(2)}) collective-permute-start(bf16[768,512]{1,0:T(8,128)(2,1)} %refs_2_.1), channel_id=1, source_target_pairs={{0,2},{1,3},{2,4},{3,5},{4,6},{5,7},{8,10},{9,11},{10,12},{11,13},... | collective-permute-start | bytes 2359304 | tf_op jit(solution)/shard_map/ppermute | solution.py:291
  8.4 2.9 %low.1 = f32[192,768]{1,0:T(8,128)} custom-call(bf16[768,512]{1,0:T(8,128)(2,1)} %x_ref, bf16[64,512]{1,0:T(8,128)(2,1)} %bitcast.20, bf16[64,512]{1,0:T(8,128)(2,1)} %bitcast.21, bf16[768,512]{1,0:T(8,128)(2,1)} %refs_2_.1, bf16[64,512]{1,0:T(8,128)(2,1)} %s_ref.1), custom_call_target="tpu_custom_call" | custom-call | flops 1024 | bytes 1024 | tf_op jit(solution)/shard_map/low/pallas_call | solution.py:171
  11.3 1.1 slice_select_fusion
  12.9 11.4 %hidden.1 = (f32[384,128]{1,0:T(8,128)}, bf16[768,2304]{1,0:T(8,128)(2,1)}, f32[768,2304]{1,0:T(8,128)}, f32[768,2304]{1,0:T(8,128)}) custom-call(bf16[768,2304]{1,0:T(8,128)(2,1)} %gate_ref.1, bf16[768,2304]{1,0:T(8,128)(2,1)} %up_ref.1, bf16[64,2304]{1,0:T(8,128)(2,1)} %bitcast.17), custom_call_target="tpu_custom_call" | custom-call | flops 1024 | bytes 1024 | tf_op jit(solution)/shard_map/hidden/pallas_call | solution.py:212
  24.7 4.4 %collective-permute-start.9 = (bf16[256,384]{1,0:T(8,128)(2,1)S(1)}, bf16[256,384]{1,0:T(8,128)(2,1)S(1)}, u32[]{:S(2)}, u32[]{:S(2)}) collective-permute-start(bf16[256,384]{1,0:T(8,128)(2,1)S(1)} %pad_maximum_fusion.1), channel_id=1, source_target_pairs={{0,2},{6,4},{1,3},{7,5},{8,10},{14,12},{9,11},{15,13},{16,18},{22,... | collective-permute-start | bytes 589832 | tf_op jit(solution)/shard_map/ppermute | solution.py:350
  29.1 1.3 collective-permute-start.3
  31.3 1.1 collective-permute-done.9
  33.6 11.2 %more.2.refs_6_ = f32[768,2304]{1,0:T(8,128)S(1)} custom-call(s32[64]{0:T(128)S(1)} %copy-done.4, s32[1]{0:T(128)} %bitcast.refs_1_, bf16[768,512]{1,0:T(8,128)(2,1)S(1)} %copy-done, bf16[768,512]{1,0:T(8,128)(2,1)S(1)} %collective-permute-done.5.refs_3_, bf16[768,512]{1,0:T(8,128)(2,1)S(1)} %broadcast_select_fusion.refs_4_, ...), custom_call_target="tpu_custom_call" | custom-call | flops 7247757312 | bytes 23592960 | tf_op jit(solution)/shard_map/more/pallas_call | solution.py:145
  44.7 4.4 %collective-permute-done.3 = bf16[768,512]{1,0:T(8,128)(2,1)S(1)} collective-permute-done((bf16[768,512]{1,0:T(8,128)(2,1)S(1)}, bf16[768,512]{1,0:T(8,128)(2,1)S(1)}, u32[]{:S(2)}, u32[]{:S(2)}) %collective-permute-start.3) | collective-permute-done | bytes 786464 | tf_op jit(solution)/shard_map/ppermute | solution.py:291
  49.6 1.3 collective-permute-start.13
  51.0 1.6 %collective-permute-start.7 = (bf16[256,512]{1,0:T(8,128)(2,1)S(1)}, bf16[256,512]{1,0:T(8,128)(2,1)S(1)}, u32[]{:S(2)}, u32[]{:S(2)}) collective-permute-start(bf16[256,512]{1,0:T(8,128)(2,1)S(1)} %broadcast_select_fusion.2), channel_id=1, source_target_pairs={{2,0},{3,1},{4,6},{5,7},{10,8},{11,9},{12,14},{13,15},{18,16},{19,... | collective-permute-start | bytes 786440 | tf_op jit(solution)/shard_map/ppermute | solution.py:289
  52.6 7.1 %more.3.refs_6_ = f32[768,2304]{1,0:T(8,128)S(1)} custom-call(s32[64]{0:T(128)S(1)} %copy-done.4, s32[1]{0:T(128)} %bitcast.refs_1_, bf16[768,512]{1,0:T(8,128)(2,1)S(1)} %select_select_fusion.refs_2_, bf16[768,512]{1,0:T(8,128)(2,1)S(1)} %collective-permute-done.8.refs_3_, bf16[2304,4096]{1,0:T(8,128)(2,1)} %refs_5_.5, bf16[2304,4096]{1,0:T(8,128)(2,1)} %refs_5_.5, ...), custom_call_target="tpu_custom_call" | custom-call | flops 3623878656 | bytes 18874368 | tf_op jit(solution)/shard_map/more/pallas_call | solution.py:145
  59.6 4.7 %collective-permute-done.7 = bf16[256,512]{1,0:T(8,128)(2,1)S(1)} collective-permute-done((bf16[256,512]{1,0:T(8,128)(2,1)S(1)}, bf16[256,512]{1,0:T(8,128)(2,1)S(1)}, u32[]{:S(2)}, u32[]{:S(2)}) %collective-permute-start.7) | collective-permute-done | bytes 262176 | tf_op jit(solution)/shard_map/ppermute | solution.py:289
  65.2 1.5 %collective-permute-start.11 = (bf16[512,512]{1,0:T(8,128)(2,1)S(1)}, bf16[512,512]{1,0:T(8,128)(2,1)S(1)}, u32[]{:S(2)}, u32[]{:S(2)}) collective-permute-start(bf16[512,512]{1,0:T(8,128)(2,1)S(1)} %broadcast_select_fusion.1), channel_id=1, source_target_pairs={{2,0},{3,1},{4,6},{5,7},{10,8},{11,9},{12,14},{13,15},{18,16},{19,... | collective-permute-start | bytes 1572872 | tf_op jit(solution)/shard_map/ppermute | solution.py:289
  67.5 1.4 %collective-permute-start.15 = (bf16[64,2304]{1,0:T(8,128)(2,1)S(1)}, bf16[64,2304]{1,0:T(8,128)(2,1)S(1)}, u32[]{:S(2)}, u32[]{:S(2)}) collective-permute-start(bf16[64,2304]{1,0:T(8,128)(2,1)S(1)} %convolution_convert_fusion), channel_id=1, source_target_pairs={{0,8},{8,0},{16,24},{24,16},{1,9},{9,1},{17,25},{25,17},{2,10},{10... | collective-permute-start | bytes 884744 | tf_op jit(solution)/shard_map/ppermute | solution.py:373
  69.0 7.3 %last_a.1 = (f32[256,128]{1,0:T(8,128)S(1)}, f32[128,2304]{1,0:T(8,128)S(1)}) custom-call(s32[64]{0:T(128)S(1)} %copy-done.4, s32[1]{0:T(128)} %bitcast.refs_1_, bf16[256,512]{1,0:T(8,128)(2,1)S(1)} %select_select_fusion.2.refs_2_, bf16[256,512]{1,0:T(8,128)(2,1)S(1)} %collective-permute-done.12.refs_3_, bf16[2304,4096]{1,0:T(8,128)(2,1)} %refs_5_.5, ...), custom_call_target="tpu_custom_call" | custom-call | flops 2415919104 | bytes 9437184 | tf_op jit(solution)/shard_map/last_a/pallas_call | solution.py:145
  76.6 4.4 %collective-permute-done.11 = bf16[512,512]{1,0:T(8,128)(2,1)S(1)} collective-permute-done((bf16[512,512]{1,0:T(8,128)(2,1)S(1)}, bf16[512,512]{1,0:T(8,128)(2,1)S(1)}, u32[]{:S(2)}, u32[]{:S(2)}) %collective-permute-start.11) | collective-permute-done | bytes 524320 | tf_op jit(solution)/shard_map/ppermute | solution.py:289
  81.9 1.4 %collective-permute-start.19 = (bf16[64,2304]{1,0:T(8,128)(2,1)S(1)}, bf16[64,2304]{1,0:T(8,128)(2,1)S(1)}, u32[]{:S(2)}, u32[]{:S(2)}) collective-permute-start(bf16[64,2304]{1,0:T(8,128)(2,1)S(1)} %add_convert_fusion.2), channel_id=1, source_target_pairs={{0,16},{8,24},{16,0},{24,8},{1,17},{9,25},{17,1},{25,9},{2,18},{10... | collective-permute-start | bytes 884744 | tf_op jit(solution)/shard_map/ppermute | solution.py:373
  83.4 11.1 %last_b.1 = (f32[512,128]{1,0:T(8,128)S(1)}, bf16[64,2304]{1,0:T(8,128)(2,1)S(1)}, bf16[64,2304]{1,0:T(8,128)(2,1)S(1)}) custom-call(s32[64]{0:T(128)S(1)} %copy-done.4, s32[1]{0:T(128)} %bitcast.refs_1_, bf16[512,512]{1,0:T(8,128)(2,1)S(1)} %select_select_fusion.1.refs_2_, bf16[512,512]{1,0:T(8,128)(2,1)S(1)} %collective-permute-done.16.refs_3_, ...), custom_call_target="tpu_custom_call" | custom-call | flops 4831838208 | bytes 14155776 | tf_op jit(solution)/shard_map/last_b/pallas_call | solution.py:145
  94.9 1.3 %collective-permute-start.21 = (bf16[64,2304]{1,0:T(8,128)(2,1)S(1)}, bf16[64,2304]{1,0:T(8,128)(2,1)S(1)}, u32[]{:S(2)}, u32[]{:S(2)}) collective-permute-start(bf16[64,2304]{1,0:T(8,128)(2,1)S(1)} %get-tuple-element.109), channel_id=1, source_target_pairs={{0,8},{8,0},{16,24},{24,16},{1,9},{9,1},{17,25},{25,17},{2,10},{10... | collective-permute-start | bytes 884744 | tf_op jit(solution)/shard_map/ppermute | solution.py:373
  96.2 1.5 %collective-permute-start.22 = (bf16[64,2304]{1,0:T(8,128)(2,1)S(1)}, bf16[64,2304]{1,0:T(8,128)(2,1)S(1)}, u32[]{:S(2)}, u32[]{:S(2)}) collective-permute-start(bf16[64,2304]{1,0:T(8,128)(2,1)S(1)} %get-tuple-element.111), channel_id=1, source_target_pairs={{0,16},{8,24},{16,0},{24,8},{1,17},{9,25},{17,1},{25,9},{2,18},{10... | collective-permute-start | bytes 884744 | tf_op jit(solution)/shard_map/ppermute | solution.py:373
  97.8 1.1 collective-permute-start.24
  98.9 2.9 %collective-permute-start.20 = (bf16[320,128]{1,0:T(8,128)(2,1)S(1)}, bf16[320,128]{1,0:T(8,128)(2,1)S(1)}, u32[]{:S(2)}, u32[]{:S(2)}) collective-permute-start(bf16[320,128]{1,0:T(8,128)(2,1)S(1)} %add_convert_fusion.4), channel_id=1, source_target_pairs={{0,4},{1,5},{2,6},{3,7},{4,0},{5,1},{6,2},{7,3},{8,12},{9,13},{10,... | collective-permute-start | bytes 245768 | tf_op jit(solution)/shard_map/ppermute | solution.py:365
  101.7 2.8 %collective-permute-done.24 = f32[256,128]{1,0:T(8,128)S(1)} collective-permute-done((f32[256,128]{1,0:T(8,128)S(1)}, f32[256,128]{1,0:T(8,128)S(1)}, u32[]{:S(2)}, u32[]{:S(2)}) %collective-permute-start.24) | collective-permute-done | bytes 131104 | tf_op jit(solution)/shard_map/ppermute | solution.py:365
  105.9 3.9 %collective-permute-start.25 = (bf16[256,128]{1,0:T(8,128)(2,1)S(1)}, bf16[256,128]{1,0:T(8,128)(2,1)S(1)}, u32[]{:S(2)}, u32[]{:S(2)}) collective-permute-start(bf16[256,128]{1,0:T(8,128)(2,1)S(1)} %add_convert_fusion.6), channel_id=1, source_target_pairs={{0,4},{1,5},{2,6},{3,7},{4,0},{5,1},{6,2},{7,3},{8,12},{9,13},{10,... | collective-permute-start | bytes 196616 | tf_op jit(solution)/shard_map/ppermute | solution.py:365
  110.6 2.1 %collective-permute-done.25 = bf16[256,128]{1,0:T(8,128)(2,1)S(1)} collective-permute-done((bf16[256,128]{1,0:T(8,128)(2,1)S(1)}, bf16[256,128]{1,0:T(8,128)(2,1)S(1)}, u32[]{:S(2)}, u32[]{:S(2)}) %collective-permute-start.25) | collective-permute-done | bytes 65568 | tf_op jit(solution)/shard_map/ppermute | solution.py:365
  114.3 3.4 %collective-permute-done.27 = bf16[64,2304]{1,0:T(8,128)(2,1)S(1)} collective-permute-done((bf16[64,2304]{1,0:T(8,128)(2,1)S(1)}, bf16[64,2304]{1,0:T(8,128)(2,1)S(1)}, u32[]{:S(2)}, u32[]{:S(2)}) %collective-permute-start.27) | collective-permute-done | bytes 294944 | tf_op jit(solution)/shard_map/ppermute | solution.py:373
  118.5 1.5 %collective-permute-start.29 = (bf16[192,512]{1,0:T(8,128)(2,1)S(1)}, bf16[192,512]{1,0:T(8,128)(2,1)S(1)}, u32[]{:S(2)}, u32[]{:S(2)}) collective-permute-start(bf16[192,512]{1,0:T(8,128)(2,1)S(1)} %fusion), channel_id=1, source_target_pairs={{0,8},{8,0},{16,24},{24,16},{1,9},{9,1},{17,25},{25,17},{2,10},{10... | collective-permute-start | bytes 589832 | tf_op jit(solution)/shard_map/ppermute | solution.py:380
  120.6 1.5 %collective-permute-start.31 = (bf16[192,512]{1,0:T(8,128)(2,1)S(1)}, bf16[192,512]{1,0:T(8,128)(2,1)S(1)}, u32[]{:S(2)}, u32[]{:S(2)}) collective-permute-start(bf16[192,512]{1,0:T(8,128)(2,1)S(1)} %fusion), channel_id=1, source_target_pairs={{0,24},{8,16},{16,8},{24,0},{1,25},{9,17},{17,9},{25,1},{2,26},{10... | collective-permute-start | bytes 589832 | tf_op jit(solution)/shard_map/ppermute | solution.py:380
  123.8 1.7 %collective-permute-done.29 = bf16[192,512]{1,0:T(8,128)(2,1)S(1)} collective-permute-done((bf16[192,512]{1,0:T(8,128)(2,1)S(1)}, bf16[192,512]{1,0:T(8,128)(2,1)S(1)}, u32[]{:S(2)}, u32[]{:S(2)}) %collective-permute-start.29) | collective-permute-done | bytes 196640 | tf_op jit(solution)/shard_map/ppermute | solution.py:380
  125.6 3.0 %collective-permute-done.30 = bf16[192,512]{1,0:T(8,128)(2,1)S(1)} collective-permute-done((bf16[192,512]{1,0:T(8,128)(2,1)S(1)}, bf16[192,512]{1,0:T(8,128)(2,1)S(1)}, u32[]{:S(2)}, u32[]{:S(2)}) %collective-permute-start.30) | collective-permute-done | bytes 196640 | tf_op jit(solution)/shard_map/ppermute | solution.py:380
  (125 shorter events, 14.2 us)
Async XLA Ops:
  0.6 23.8 %collective-permute-start = (bf16[768,512]{1,0:T(8,128)(2,1)}, bf16[768,512]{1,0:T(8,128)(2,1)S(1)}, u32[]{:S(2)}, u32[]{:S(2)}) collective-permute-start(bf16[768,512]{1,0:T(8,128)(2,1)} %refs_2_.1), channel_id=1, source_target_pairs={{2,0},{3,1},{4,2},{5,3},{6,4},{7,5},{10,8},{11,9},{12,10},{13,11},... | collective-permute-start | bytes 2359304 | tf_op jit(solution)/shard_map/ppermute | solution.py:291
  1.9 22.7 %collective-permute-start.1 = (bf16[768,512]{1,0:T(8,128)(2,1)}, bf16[768,512]{1,0:T(8,128)(2,1)}, u32[]{:S(2)}, u32[]{:S(2)}) collective-permute-start(bf16[768,512]{1,0:T(8,128)(2,1)} %refs_2_.1), channel_id=1, source_target_pairs={{0,2},{1,3},{2,4},{3,5},{4,6},{5,7},{8,10},{9,11},{10,12},{11,13},... | collective-permute-start | bytes 2359304 | tf_op jit(solution)/shard_map/ppermute | solution.py:291
  12.3 12.0 %collective-permute-start.2 = (f32[192,384]{1,0:T(8,128)S(1)}, f32[192,384]{1,0:T(8,128)S(1)}, u32[]{:S(2)}, u32[]{:S(2)}) collective-permute-start(f32[192,384]{1,0:T(8,128)S(1)} %slice_select_fusion), channel_id=1, source_target_pairs={{0,1},{1,0},{2,3},{3,2},{4,5},{5,4},{6,7},{7,6},{8,9},{9,8},{10,11... | collective-permute-start | bytes 884744 | tf_op jit(solution)/shard_map/ppermute | solution.py:311
  12.4 20.9 %collective-permute-start.5 = (bf16[768,512]{1,0:T(8,128)(2,1)}, bf16[768,512]{1,0:T(8,128)(2,1)S(1)}, u32[]{:S(2)}, u32[]{:S(2)}) collective-permute-start(bf16[768,512]{1,0:T(8,128)(2,1)} %refs_2_.1), channel_id=1, source_target_pairs={{0,1},{1,0},{2,3},{3,2},{4,5},{5,4},{6,7},{7,6},{8,9},{9,8},{10,11... | collective-permute-start | bytes 2359304 | tf_op jit(solution)/shard_map/ppermute | solution.py:311
  24.7 7.7 %collective-permute-start.9 = (bf16[256,384]{1,0:T(8,128)(2,1)S(1)}, bf16[256,384]{1,0:T(8,128)(2,1)S(1)}, u32[]{:S(2)}, u32[]{:S(2)}) collective-permute-start(bf16[256,384]{1,0:T(8,128)(2,1)S(1)} %pad_maximum_fusion.1), channel_id=1, source_target_pairs={{0,2},{6,4},{1,3},{7,5},{8,10},{14,12},{9,11},{15,13},{16,18},{22,... | collective-permute-start | bytes 589832 | tf_op jit(solution)/shard_map/ppermute | solution.py:350
  29.1 20.0 %collective-permute-start.3 = (bf16[768,512]{1,0:T(8,128)(2,1)S(1)}, bf16[768,512]{1,0:T(8,128)(2,1)S(1)}, u32[]{:S(2)}, u32[]{:S(2)}) collective-permute-start(bf16[768,512]{1,0:T(8,128)(2,1)S(1)} %collective-permute-done), channel_id=1, source_target_pairs={{2,0},{3,1},{4,2},{5,3},{10,8},{11,9},{12,10},{13,11},{18,16},{19,... | collective-permute-start | bytes 2359304 | tf_op jit(solution)/shard_map/ppermute | solution.py:291
  30.4 18.7 %collective-permute-start.4 = (bf16[768,512]{1,0:T(8,128)(2,1)}, bf16[768,512]{1,0:T(8,128)(2,1)S(1)}, u32[]{:S(2)}, u32[]{:S(2)}) collective-permute-start(bf16[768,512]{1,0:T(8,128)(2,1)} %collective-permute-done.1), channel_id=1, source_target_pairs={{2,4},{3,5},{4,6},{5,7},{10,12},{11,13},{12,14},{13,15},{18,20},{1... | collective-permute-start | bytes 2359304 | tf_op jit(solution)/shard_map/ppermute | solution.py:291
  31.2 2.4 %collective-permute-start.6 = (bf16[768,512]{1,0:T(8,128)(2,1)S(1)}, bf16[768,512]{1,0:T(8,128)(2,1)S(1)}, u32[]{:S(2)}, u32[]{:S(2)}) collective-permute-start(bf16[768,512]{1,0:T(8,128)(2,1)S(1)} %broadcast_select_fusion.refs_4_), channel_id=1, source_target_pairs={{0,1},{1,0},{2,3},{3,2},{4,5},{5,4},{6,7},{7,6},{8,9},{9,8},{10,11... | collective-permute-start | bytes 2359304 | tf_op jit(solution)/shard_map/ppermute | solution.py:311
  32.5 16.8 %collective-permute-start.10 = (bf16[256,384]{1,0:T(8,128)(2,1)S(1)}, bf16[256,384]{1,0:T(8,128)(2,1)S(1)}, u32[]{:S(2)}, u32[]{:S(2)}) collective-permute-start(bf16[256,384]{1,0:T(8,128)(2,1)S(1)} %pad_maximum_fusion.2), channel_id=1, source_target_pairs={{2,4},{4,2},{3,5},{5,3},{10,12},{12,10},{11,13},{13,11},{18,20},{2... | collective-permute-start | bytes 589832 | tf_op jit(solution)/shard_map/ppermute | solution.py:350
  49.2 3.3 %collective-permute-start.8 = (bf16[768,512]{1,0:T(8,128)(2,1)S(1)}, bf16[768,512]{1,0:T(8,128)(2,1)S(1)}, u32[]{:S(2)}, u32[]{:S(2)}) collective-permute-start(bf16[768,512]{1,0:T(8,128)(2,1)S(1)} %select_select_fusion.refs_2_), channel_id=1, source_target_pairs={{0,1},{1,0},{2,3},{3,2},{4,5},{5,4},{6,7},{7,6},{8,9},{9,8},{10,11... | collective-permute-start | bytes 2359304 | tf_op jit(solution)/shard_map/ppermute | solution.py:311
  49.6 14.7 %collective-permute-start.13 = (bf16[192,384]{1,0:T(8,128)(2,1)S(1)}, bf16[192,384]{1,0:T(8,128)(2,1)S(1)}, u32[]{:S(2)}, u32[]{:S(2)}) collective-permute-start(bf16[192,384]{1,0:T(8,128)(2,1)S(1)} %fusion.1), channel_id=1, source_target_pairs={{2,0},{4,6},{3,1},{5,7},{10,8},{12,14},{11,9},{13,15},{18,16},{20,... | collective-permute-start | bytes 442376 | tf_op jit(solution)/shard_map/ppermute | solution.py:350
  51.0 13.4 %collective-permute-start.7 = (bf16[256,512]{1,0:T(8,128)(2,1)S(1)}, bf16[256,512]{1,0:T(8,128)(2,1)S(1)}, u32[]{:S(2)}, u32[]{:S(2)}) collective-permute-start(bf16[256,512]{1,0:T(8,128)(2,1)S(1)} %broadcast_select_fusion.2), channel_id=1, source_target_pairs={{2,0},{3,1},{4,6},{5,7},{10,8},{11,9},{12,14},{13,15},{18,16},{19,... | collective-permute-start | bytes 786440 | tf_op jit(solution)/shard_map/ppermute | solution.py:289
  64.4 2.3 %collective-permute-start.14 = (bf16[192,384]{1,0:T(8,128)(2,1)S(1)}, bf16[192,384]{1,0:T(8,128)(2,1)S(1)}, u32[]{:S(2)}, u32[]{:S(2)}) collective-permute-start(bf16[192,384]{1,0:T(8,128)(2,1)S(1)} %broadcast_select_fusion.3), channel_id=1, source_target_pairs={{0,1},{1,0},{2,3},{3,2},{4,5},{5,4},{6,7},{7,6},{8,9},{9,8},{10,11... | collective-permute-start | bytes 442376 | tf_op jit(solution)/shard_map/ppermute | solution.py:311
  64.6 4.4 %collective-permute-start.12 = (bf16[256,512]{1,0:T(8,128)(2,1)S(1)}, bf16[256,512]{1,0:T(8,128)(2,1)S(1)}, u32[]{:S(2)}, u32[]{:S(2)}) collective-permute-start(bf16[256,512]{1,0:T(8,128)(2,1)S(1)} %select_select_fusion.2.refs_2_), channel_id=1, source_target_pairs={{0,1},{1,0},{2,3},{3,2},{4,5},{5,4},{6,7},{7,6},{8,9},{9,8},{10,11... | collective-permute-start | bytes 786440 | tf_op jit(solution)/shard_map/ppermute | solution.py:311
  65.2 15.9 %collective-permute-start.11 = (bf16[512,512]{1,0:T(8,128)(2,1)S(1)}, bf16[512,512]{1,0:T(8,128)(2,1)S(1)}, u32[]{:S(2)}, u32[]{:S(2)}) collective-permute-start(bf16[512,512]{1,0:T(8,128)(2,1)S(1)} %broadcast_select_fusion.1), channel_id=1, source_target_pairs={{2,0},{3,1},{4,6},{5,7},{10,8},{11,9},{12,14},{13,15},{18,16},{19,... | collective-permute-start | bytes 1572872 | tf_op jit(solution)/shard_map/ppermute | solution.py:289
  67.5 9.1 %collective-permute-start.15 = (bf16[64,2304]{1,0:T(8,128)(2,1)S(1)}, bf16[64,2304]{1,0:T(8,128)(2,1)S(1)}, u32[]{:S(2)}, u32[]{:S(2)}) collective-permute-start(bf16[64,2304]{1,0:T(8,128)(2,1)S(1)} %convolution_convert_fusion), channel_id=1, source_target_pairs={{0,8},{8,0},{16,24},{24,16},{1,9},{9,1},{17,25},{25,17},{2,10},{10... | collective-permute-start | bytes 884744 | tf_op jit(solution)/shard_map/ppermute | solution.py:373
  81.1 2.2 %collective-permute-start.17 = (f32[320,128]{1,0:T(8,128)S(1)}, f32[320,128]{1,0:T(8,128)S(1)}, u32[]{:S(2)}, u32[]{:S(2)}) collective-permute-start(f32[320,128]{1,0:T(8,128)S(1)} %fusion.11), channel_id=1, source_target_pairs={{0,1},{1,0},{2,3},{3,2},{4,5},{5,4},{6,7},{7,6},{8,9},{9,8},{10,11... | collective-permute-start | bytes 491528 | tf_op jit(solution)/shard_map/ppermute | solution.py:311
  81.2 2.2 %collective-permute-start.16 = (bf16[512,512]{1,0:T(8,128)(2,1)S(1)}, bf16[512,512]{1,0:T(8,128)(2,1)S(1)}, u32[]{:S(2)}, u32[]{:S(2)}) collective-permute-start(bf16[512,512]{1,0:T(8,128)(2,1)S(1)} %select_select_fusion.1.refs_2_), channel_id=1, source_target_pairs={{0,1},{1,0},{2,3},{3,2},{4,5},{5,4},{6,7},{7,6},{8,9},{9,8},{10,11... | collective-permute-start | bytes 1572872 | tf_op jit(solution)/shard_map/ppermute | solution.py:311
  81.9 12.6 %collective-permute-start.19 = (bf16[64,2304]{1,0:T(8,128)(2,1)S(1)}, bf16[64,2304]{1,0:T(8,128)(2,1)S(1)}, u32[]{:S(2)}, u32[]{:S(2)}) collective-permute-start(bf16[64,2304]{1,0:T(8,128)(2,1)S(1)} %add_convert_fusion.2), channel_id=1, source_target_pairs={{0,16},{8,24},{16,0},{24,8},{1,17},{9,25},{17,1},{25,9},{2,18},{10... | collective-permute-start | bytes 884744 | tf_op jit(solution)/shard_map/ppermute | solution.py:373
  83.3 11.2 %collective-permute-start.18 = (f32[320,128]{1,0:T(8,128)S(1)}, f32[320,128]{1,0:T(8,128)S(1)}, u32[]{:S(2)}, u32[]{:S(2)}) collective-permute-start(f32[320,128]{1,0:T(8,128)S(1)} %select_add_fusion.1), channel_id=1, source_target_pairs={{0,2},{1,3},{2,0},{3,1},{4,6},{5,7},{6,4},{7,5},{8,10},{9,11},{10,... | collective-permute-start | bytes 491528 | tf_op jit(solution)/shard_map/ppermute | solution.py:365
  94.5 3.2 %collective-permute-start.23 = (f32[256,128]{1,0:T(8,128)S(1)}, f32[256,128]{1,0:T(8,128)S(1)}, u32[]{:S(2)}, u32[]{:S(2)}) collective-permute-start(f32[256,128]{1,0:T(8,128)S(1)} %slice_select_fusion.1), channel_id=1, source_target_pairs={{0,1},{1,0},{2,3},{3,2},{4,5},{5,4},{6,7},{7,6},{8,9},{9,8},{10,11... | collective-permute-start | bytes 393224 | tf_op jit(solution)/shard_map/ppermute | solution.py:311
  94.9 9.7 %collective-permute-start.21 = (bf16[64,2304]{1,0:T(8,128)(2,1)S(1)}, bf16[64,2304]{1,0:T(8,128)(2,1)S(1)}, u32[]{:S(2)}, u32[]{:S(2)}) collective-permute-start(bf16[64,2304]{1,0:T(8,128)(2,1)S(1)} %get-tuple-element.109), channel_id=1, source_target_pairs={{0,8},{8,0},{16,24},{24,16},{1,9},{9,1},{17,25},{25,17},{2,10},{10... | collective-permute-start | bytes 884744 | tf_op jit(solution)/shard_map/ppermute | solution.py:373
  96.2 9.1 %collective-permute-start.22 = (bf16[64,2304]{1,0:T(8,128)(2,1)S(1)}, bf16[64,2304]{1,0:T(8,128)(2,1)S(1)}, u32[]{:S(2)}, u32[]{:S(2)}) collective-permute-start(bf16[64,2304]{1,0:T(8,128)(2,1)S(1)} %get-tuple-element.111), channel_id=1, source_target_pairs={{0,16},{8,24},{16,0},{24,8},{1,17},{9,25},{17,1},{25,9},{2,18},{10... | collective-permute-start | bytes 884744 | tf_op jit(solution)/shard_map/ppermute | solution.py:373
  97.8 6.8 %collective-permute-start.24 = (f32[256,128]{1,0:T(8,128)S(1)}, f32[256,128]{1,0:T(8,128)S(1)}, u32[]{:S(2)}, u32[]{:S(2)}) collective-permute-start(f32[256,128]{1,0:T(8,128)S(1)} %select_add_fusion.2), channel_id=1, source_target_pairs={{0,2},{1,3},{2,0},{3,1},{4,6},{5,7},{6,4},{7,5},{8,10},{9,11},{10,... | collective-permute-start | bytes 393224 | tf_op jit(solution)/shard_map/ppermute | solution.py:365
  98.9 11.8 %collective-permute-start.20 = (bf16[320,128]{1,0:T(8,128)(2,1)S(1)}, bf16[320,128]{1,0:T(8,128)(2,1)S(1)}, u32[]{:S(2)}, u32[]{:S(2)}) collective-permute-start(bf16[320,128]{1,0:T(8,128)(2,1)S(1)} %add_convert_fusion.4), channel_id=1, source_target_pairs={{0,4},{1,5},{2,6},{3,7},{4,0},{5,1},{6,2},{7,3},{8,12},{9,13},{10,... | collective-permute-start | bytes 245768 | tf_op jit(solution)/shard_map/ppermute | solution.py:365
  105.3 8.9 %collective-permute-start.28 = (bf16[64,2304]{1,0:T(8,128)(2,1)S(1)}, bf16[64,2304]{1,0:T(8,128)(2,1)S(1)}, u32[]{:S(2)}, u32[]{:S(2)}) collective-permute-start(bf16[64,2304]{1,0:T(8,128)(2,1)S(1)} %add_convert_fusion), channel_id=1, source_target_pairs={{0,8},{8,0},{16,24},{24,16},{1,9},{9,1},{17,25},{25,17},{2,10},{10... | collective-permute-start | bytes 884744 | tf_op jit(solution)/shard_map/ppermute | solution.py:373
  105.9 6.8 %collective-permute-start.25 = (bf16[256,128]{1,0:T(8,128)(2,1)S(1)}, bf16[256,128]{1,0:T(8,128)(2,1)S(1)}, u32[]{:S(2)}, u32[]{:S(2)}) collective-permute-start(bf16[256,128]{1,0:T(8,128)(2,1)S(1)} %add_convert_fusion.6), channel_id=1, source_target_pairs={{0,4},{1,5},{2,6},{3,7},{4,0},{5,1},{6,2},{7,3},{8,12},{9,13},{10,... | collective-permute-start | bytes 196616 | tf_op jit(solution)/shard_map/ppermute | solution.py:365
  109.9 7.8 %collective-permute-start.27 = (bf16[64,2304]{1,0:T(8,128)(2,1)S(1)}, bf16[64,2304]{1,0:T(8,128)(2,1)S(1)}, u32[]{:S(2)}, u32[]{:S(2)}) collective-permute-start(bf16[64,2304]{1,0:T(8,128)(2,1)S(1)} %add_convert_fusion.1), channel_id=1, source_target_pairs={{0,16},{8,24},{16,0},{24,8},{1,17},{9,25},{17,1},{25,9},{2,18},{10... | collective-permute-start | bytes 884744 | tf_op jit(solution)/shard_map/ppermute | solution.py:373
  112.8 1.4 %collective-permute-start.26 = (bf16[576,128]{1,0:T(8,128)(2,1)S(1)}, bf16[576,128]{1,0:T(8,128)(2,1)S(1)}, u32[]{:S(2)}, u32[]{:S(2)}) collective-permute-start(bf16[576,128]{1,0:T(8,128)(2,1)S(1)} %pad_maximum_fusion.5), channel_id=1, source_target_pairs={{0,1},{1,0},{2,3},{3,2},{4,5},{5,4},{6,7},{7,6},{8,9},{9,8},{10,11... | collective-permute-start | bytes 442376 | tf_op jit(solution)/shard_map/ppermute | solution.py:311
  118.5 7.1 %collective-permute-start.29 = (bf16[192,512]{1,0:T(8,128)(2,1)S(1)}, bf16[192,512]{1,0:T(8,128)(2,1)S(1)}, u32[]{:S(2)}, u32[]{:S(2)}) collective-permute-start(bf16[192,512]{1,0:T(8,128)(2,1)S(1)} %fusion), channel_id=1, source_target_pairs={{0,8},{8,0},{16,24},{24,16},{1,9},{9,1},{17,25},{25,17},{2,10},{10... | collective-permute-start | bytes 589832 | tf_op jit(solution)/shard_map/ppermute | solution.py:380
  120.0 8.6 %collective-permute-start.30 = (bf16[192,512]{1,0:T(8,128)(2,1)S(1)}, bf16[192,512]{1,0:T(8,128)(2,1)S(1)}, u32[]{:S(2)}, u32[]{:S(2)}) collective-permute-start(bf16[192,512]{1,0:T(8,128)(2,1)S(1)} %fusion), channel_id=1, source_target_pairs={{0,16},{8,24},{16,0},{24,8},{1,17},{9,25},{17,1},{25,9},{2,18},{10... | collective-permute-start | bytes 589832 | tf_op jit(solution)/shard_map/ppermute | solution.py:380
  120.6 8.0 %collective-permute-start.31 = (bf16[192,512]{1,0:T(8,128)(2,1)S(1)}, bf16[192,512]{1,0:T(8,128)(2,1)S(1)}, u32[]{:S(2)}, u32[]{:S(2)}) collective-permute-start(bf16[192,512]{1,0:T(8,128)(2,1)S(1)} %fusion), channel_id=1, source_target_pairs={{0,24},{8,16},{16,8},{24,0},{1,25},{9,17},{17,9},{25,1},{2,26},{10... | collective-permute-start | bytes 589832 | tf_op jit(solution)/shard_map/ppermute | solution.py:380
  (11 other events, 125.0 us)

commit v2 on v1

--- a/solution.py
+++ b/solution.py
@@ -485,19 +485,15 @@
     half = part_b.shape[0] // 2
     after = places.meet(part_b[:half], part_b[half:])
     across = places.send_across(after, 1)
-    before = summed(before)
     k = 2
     while k < places.chips:
-        beside = places.send_across(before, k)
-        sent, across = barrier((sent, across))
-        if k == 2:
-            large = [summed(pair) for pair in sent]
-            sent = [places.dp_send(x, order[1]) for x, order in zip(large, bits)]
+        before, across = barrier((before, across))
+        before = places.send_across(summed(before), k)
         across = places.send_across(summed(across), k)
-        beside, across = barrier((beside, across))
-        before = summed(beside)
         k *= 2
-    total = jnp.concatenate([before, summed(across)], axis=0).astype(BF)
+    large = [summed(pair) for pair in sent]
+    sent = [places.dp_send(x, order[1]) for x, order in zip(large, bits)]
+    total = jnp.concatenate([summed(before), summed(across)], axis=0).astype(BF)
     other, sent = barrier((places.swap(total), sent))
     large = [summed(pair) for pair in sent]
     sums = places.order(total, other)

time: 130 us -> 128 us (0.985)
  starting transfers between devices: 40.1 us -> 38.1 us
    ppermute x4, starting transfers between devices: 7.93 us -> 5.83 us  [send_across(): return (mine, lax.ppermute(mine, 'tensor', pairs))]
  transfers between devices with their start and end apart: 32 -> 32, of which waited for: 14 -> 16; matrix products, arithmetic and copies ran while one was open for 4% -> 5% of each run, Pallas kernels for 39% -> 40%
where the time goes in v2:
time: 128 us
  Pallas kernels  50.8 us (40%)
  starting transfers between devices  38.1 us (30%)
  waiting for transfers between devices  29.8 us (23%)
  other arithmetic  5.15 us (4%)
  between operations  1.4 us (1%)
    pallas_call x4, Pallas kernels, grad_call(): pl.pallas_call(functools.partial(grad_kernel, len(blocks), acc is not Non...  36.5 us
    pallas_call x1, Pallas kernels, hidden_call(): pl.pallas_call(hidden_kernel, grid=(hidden // tile,), in_specs=[wide, wid...  11.4 us
    ppermute x2, waiting for transfers between devices, flood(): both = lax.ppermute(chosen, 'tensor', pairs[0] + pairs[1])  9.16 us
    ppermute x2, starting transfers between devices, flood(): lax.ppermute(down, 'tensor', pairs[1])  7.16 us
    ppermute x6, starting transfers between devices, dp_send(): lax.ppermute(mine, 'dp', [(i, i ^ bit) for i in range(self.dps)])  7.11 us
    ppermute x3, starting transfers between devices, low_send(): return (mine, lax.ppermute(mine, 'tensor', pairs))  6.49 us
    ppermute x4, starting transfers between devices, send_across(): return (mine, lax.ppermute(mine, 'tensor', pairs))  5.83 us
    ppermute x4, waiting for transfers between devices, send_across(): return (mine, lax.ppermute(mine, 'tensor', pairs))  4.53 us
  transfers between devices with their start and end apart: 32, of which 16 were waited for; matrix products, arithmetic and copies ran while one was open for 5% of the time, Pallas kernels for 40%

profile of v2, /device:TPU:0, one launch (start us, length us, event | category | flops | bytes accessed | tf_op | source)
XLA Modules:
  0.0 127.7 jit_solution(12166994659429763085)
XLA Ops:
  0.6 1.3 %collective-permute-start = (bf16[768,512]{1,0:T(8,128)(2,1)}, bf16[768,512]{1,0:T(8,128)(2,1)S(1)}, u32[]{:S(2)}, u32[]{:S(2)}) collective-permute-start(bf16[768,512]{1,0:T(8,128)(2,1)} %refs_2_.1), channel_id=1, source_target_pairs={{2,0},{3,1},{4,2},{5,3},{6,4},{7,5},{10,8},{11,9},{12,10},{13,11},... | collective-permute-start | bytes 2359304 | tf_op jit(solution)/shard_map/ppermute | solution.py:291
  1.9 6.4 %collective-permute-start.1 = (bf16[768,512]{1,0:T(8,128)(2,1)}, bf16[768,512]{1,0:T(8,128)(2,1)}, u32[]{:S(2)}, u32[]{:S(2)}) collective-permute-start(bf16[768,512]{1,0:T(8,128)(2,1)} %refs_2_.1), channel_id=1, source_target_pairs={{0,2},{1,3},{2,4},{3,5},{4,6},{5,7},{8,10},{9,11},{10,12},{11,13},... | collective-permute-start | bytes 2359304 | tf_op jit(solution)/shard_map/ppermute | solution.py:291
  8.4 2.9 %low.1 = f32[192,768]{1,0:T(8,128)} custom-call(bf16[768,512]{1,0:T(8,128)(2,1)} %x_ref, bf16[64,512]{1,0:T(8,128)(2,1)} %bitcast.20, bf16[64,512]{1,0:T(8,128)(2,1)} %bitcast.21, bf16[768,512]{1,0:T(8,128)(2,1)} %refs_2_.1, bf16[64,512]{1,0:T(8,128)(2,1)} %s_ref.1), custom_call_target="tpu_custom_call" | custom-call | flops 1024 | bytes 1024 | tf_op jit(solution)/shard_map/low/pallas_call | solution.py:171
  11.3 1.1 slice_select_fusion
  12.9 11.4 %hidden.1 = (f32[384,128]{1,0:T(8,128)}, bf16[768,2304]{1,0:T(8,128)(2,1)}, f32[768,2304]{1,0:T(8,128)}, f32[768,2304]{1,0:T(8,128)}) custom-call(bf16[768,2304]{1,0:T(8,128)(2,1)} %gate_ref.1, bf16[768,2304]{1,0:T(8,128)(2,1)} %up_ref.1, bf16[64,2304]{1,0:T(8,128)(2,1)} %bitcast.17), custom_call_target="tpu_custom_call" | custom-call | flops 1024 | bytes 1024 | tf_op jit(solution)/shard_map/hidden/pallas_call | solution.py:212
  24.7 4.4 %collective-permute-start.9 = (bf16[256,384]{1,0:T(8,128)(2,1)S(1)}, bf16[256,384]{1,0:T(8,128)(2,1)S(1)}, u32[]{:S(2)}, u32[]{:S(2)}) collective-permute-start(bf16[256,384]{1,0:T(8,128)(2,1)S(1)} %pad_maximum_fusion.1), channel_id=1, source_target_pairs={{0,2},{6,4},{1,3},{7,5},{8,10},{14,12},{9,11},{15,13},{16,18},{22,... | collective-permute-start | bytes 589832 | tf_op jit(solution)/shard_map/ppermute | solution.py:350
  29.1 1.3 %collective-permute-start.3 = (bf16[768,512]{1,0:T(8,128)(2,1)S(1)}, bf16[768,512]{1,0:T(8,128)(2,1)S(1)}, u32[]{:S(2)}, u32[]{:S(2)}) collective-permute-start(bf16[768,512]{1,0:T(8,128)(2,1)S(1)} %collective-permute-done), channel_id=1, source_target_pairs={{2,0},{3,1},{4,2},{5,3},{10,8},{11,9},{12,10},{13,11},{18,16},{19,... | collective-permute-start | bytes 2359304 | tf_op jit(solution)/shard_map/ppermute | solution.py:291
  33.6 11.2 %more.2.refs_6_ = f32[768,2304]{1,0:T(8,128)S(1)} custom-call(s32[64]{0:T(128)S(1)} %copy-done.4, s32[1]{0:T(128)} %bitcast.refs_1_, bf16[768,512]{1,0:T(8,128)(2,1)S(1)} %copy-done, bf16[768,512]{1,0:T(8,128)(2,1)S(1)} %collective-permute-done.5.refs_3_, bf16[768,512]{1,0:T(8,128)(2,1)S(1)} %broadcast_select_fusion.refs_4_, ...), custom_call_target="tpu_custom_call" | custom-call | flops 7247757312 | bytes 23592960 | tf_op jit(solution)/shard_map/more/pallas_call | solution.py:145
  44.7 4.4 %collective-permute-done.3 = bf16[768,512]{1,0:T(8,128)(2,1)S(1)} collective-permute-done((bf16[768,512]{1,0:T(8,128)(2,1)S(1)}, bf16[768,512]{1,0:T(8,128)(2,1)S(1)}, u32[]{:S(2)}, u32[]{:S(2)}) %collective-permute-start.3) | collective-permute-done | bytes 786464 | tf_op jit(solution)/shard_map/ppermute | solution.py:291
  49.6 1.3 %collective-permute-start.13 = (bf16[192,384]{1,0:T(8,128)(2,1)S(1)}, bf16[192,384]{1,0:T(8,128)(2,1)S(1)}, u32[]{:S(2)}, u32[]{:S(2)}) collective-permute-start(bf16[192,384]{1,0:T(8,128)(2,1)S(1)} %fusion.1), channel_id=1, source_target_pairs={{2,0},{4,6},{3,1},{5,7},{10,8},{12,14},{11,9},{13,15},{18,16},{20,... | collective-permute-start | bytes 442376 | tf_op jit(solution)/shard_map/ppermute | solution.py:350
  51.0 1.6 %collective-permute-start.7 = (bf16[256,512]{1,0:T(8,128)(2,1)S(1)}, bf16[256,512]{1,0:T(8,128)(2,1)S(1)}, u32[]{:S(2)}, u32[]{:S(2)}) collective-permute-start(bf16[256,512]{1,0:T(8,128)(2,1)S(1)} %broadcast_select_fusion.2), channel_id=1, source_target_pairs={{2,0},{3,1},{4,6},{5,7},{10,8},{11,9},{12,14},{13,15},{18,16},{19,... | collective-permute-start | bytes 786440 | tf_op jit(solution)/shard_map/ppermute | solution.py:289
  52.6 7.1 %more.3.refs_6_ = f32[768,2304]{1,0:T(8,128)S(1)} custom-call(s32[64]{0:T(128)S(1)} %copy-done.4, s32[1]{0:T(128)} %bitcast.refs_1_, bf16[768,512]{1,0:T(8,128)(2,1)S(1)} %select_select_fusion.refs_2_, bf16[768,512]{1,0:T(8,128)(2,1)S(1)} %collective-permute-done.8.refs_3_, bf16[2304,4096]{1,0:T(8,128)(2,1)} %refs_5_.5, bf16[2304,4096]{1,0:T(8,128)(2,1)} %refs_5_.5, ...), custom_call_target="tpu_custom_call" | custom-call | flops 3623878656 | bytes 18874368 | tf_op jit(solution)/shard_map/more/pallas_call | solution.py:145
  59.6 4.7 %collective-permute-done.7 = bf16[256,512]{1,0:T(8,128)(2,1)S(1)} collective-permute-done((bf16[256,512]{1,0:T(8,128)(2,1)S(1)}, bf16[256,512]{1,0:T(8,128)(2,1)S(1)}, u32[]{:S(2)}, u32[]{:S(2)}) %collective-permute-start.7) | collective-permute-done | bytes 262176 | tf_op jit(solution)/shard_map/ppermute | solution.py:289
  65.2 1.5 %collective-permute-start.11 = (bf16[512,512]{1,0:T(8,128)(2,1)S(1)}, bf16[512,512]{1,0:T(8,128)(2,1)S(1)}, u32[]{:S(2)}, u32[]{:S(2)}) collective-permute-start(bf16[512,512]{1,0:T(8,128)(2,1)S(1)} %broadcast_select_fusion.1), channel_id=1, source_target_pairs={{2,0},{3,1},{4,6},{5,7},{10,8},{11,9},{12,14},{13,15},{18,16},{19,... | collective-permute-start | bytes 1572872 | tf_op jit(solution)/shard_map/ppermute | solution.py:289
  67.5 1.4 %collective-permute-start.15 = (bf16[64,2304]{1,0:T(8,128)(2,1)S(1)}, bf16[64,2304]{1,0:T(8,128)(2,1)S(1)}, u32[]{:S(2)}, u32[]{:S(2)}) collective-permute-start(bf16[64,2304]{1,0:T(8,128)(2,1)S(1)} %convolution_convert_fusion), channel_id=1, source_target_pairs={{0,8},{8,0},{16,24},{24,16},{1,9},{9,1},{17,25},{25,17},{2,10},{10... | collective-permute-start | bytes 884744 | tf_op jit(solution)/shard_map/ppermute | solution.py:373
  69.0 7.3 %last_a.1 = (f32[256,128]{1,0:T(8,128)S(1)}, f32[128,2304]{1,0:T(8,128)S(1)}) custom-call(s32[64]{0:T(128)S(1)} %copy-done.4, s32[1]{0:T(128)} %bitcast.refs_1_, bf16[256,512]{1,0:T(8,128)(2,1)S(1)} %select_select_fusion.2.refs_2_, bf16[256,512]{1,0:T(8,128)(2,1)S(1)} %collective-permute-done.12.refs_3_, bf16[2304,4096]{1,0:T(8,128)(2,1)} %refs_5_.5, ...), custom_call_target="tpu_custom_call" | custom-call | flops 2415919104 | bytes 9437184 | tf_op jit(solution)/shard_map/last_a/pallas_call | solution.py:145
  76.6 4.4 %collective-permute-done.11 = bf16[512,512]{1,0:T(8,128)(2,1)S(1)} collective-permute-done((bf16[512,512]{1,0:T(8,128)(2,1)S(1)}, bf16[512,512]{1,0:T(8,128)(2,1)S(1)}, u32[]{:S(2)}, u32[]{:S(2)}) %collective-permute-start.11) | collective-permute-done | bytes 524320 | tf_op jit(solution)/shard_map/ppermute | solution.py:289
  81.9 1.4 %collective-permute-start.19 = (bf16[64,2304]{1,0:T(8,128)(2,1)S(1)}, bf16[64,2304]{1,0:T(8,128)(2,1)S(1)}, u32[]{:S(2)}, u32[]{:S(2)}) collective-permute-start(bf16[64,2304]{1,0:T(8,128)(2,1)S(1)} %add_convert_fusion.2), channel_id=1, source_target_pairs={{0,16},{8,24},{16,0},{24,8},{1,17},{9,25},{17,1},{25,9},{2,18},{10... | collective-permute-start | bytes 884744 | tf_op jit(solution)/shard_map/ppermute | solution.py:373
  83.4 11.1 %last_b.1 = (f32[512,128]{1,0:T(8,128)S(1)}, bf16[64,2304]{1,0:T(8,128)(2,1)S(1)}, bf16[64,2304]{1,0:T(8,128)(2,1)S(1)}) custom-call(s32[64]{0:T(128)S(1)} %copy-done.4, s32[1]{0:T(128)} %bitcast.refs_1_, bf16[512,512]{1,0:T(8,128)(2,1)S(1)} %select_select_fusion.1.refs_2_, bf16[512,512]{1,0:T(8,128)(2,1)S(1)} %collective-permute-done.16.refs_3_, ...), custom_call_target="tpu_custom_call" | custom-call | flops 4831838208 | bytes 14155776 | tf_op jit(solution)/shard_map/last_b/pallas_call | solution.py:145
  94.9 1.1 collective-permute-done.20
  96.0 2.1 %collective-permute-start.21 = (f32[256,128]{1,0:T(8,128)S(1)}, f32[256,128]{1,0:T(8,128)S(1)}, u32[]{:S(2)}, u32[]{:S(2)}) collective-permute-start(f32[256,128]{1,0:T(8,128)S(1)} %select_add_fusion.2), channel_id=1, source_target_pairs={{0,2},{1,3},{2,0},{3,1},{4,6},{5,7},{6,4},{7,5},{8,10},{9,11},{10,... | collective-permute-start | bytes 393224 | tf_op jit(solution)/shard_map/ppermute | solution.py:365
  98.7 1.4 %collective-permute-start.25 = (bf16[64,2304]{1,0:T(8,128)(2,1)S(1)}, bf16[64,2304]{1,0:T(8,128)(2,1)S(1)}, u32[]{:S(2)}, u32[]{:S(2)}) collective-permute-start(bf16[64,2304]{1,0:T(8,128)(2,1)S(1)} %get-tuple-element.99), channel_id=1, source_target_pairs={{0,8},{8,0},{16,24},{24,16},{1,9},{9,1},{17,25},{25,17},{2,10},{10... | collective-permute-start | bytes 884744 | tf_op jit(solution)/shard_map/ppermute | solution.py:373
  100.1 1.7 %collective-permute-done.21 = f32[256,128]{1,0:T(8,128)S(1)} collective-permute-done((f32[256,128]{1,0:T(8,128)S(1)}, f32[256,128]{1,0:T(8,128)S(1)}, u32[]{:S(2)}, u32[]{:S(2)}) %collective-permute-start.21) | collective-permute-done | bytes 131104 | tf_op jit(solution)/shard_map/ppermute | solution.py:365
  101.9 3.6 %collective-permute-start.22 = (bf16[320,128]{1,0:T(8,128)(2,1)S(1)}, bf16[320,128]{1,0:T(8,128)(2,1)S(1)}, u32[]{:S(2)}, u32[]{:S(2)}) collective-permute-start(bf16[320,128]{1,0:T(8,128)(2,1)S(1)} %add_convert_fusion.4), channel_id=1, source_target_pairs={{0,4},{1,5},{2,6},{3,7},{4,0},{5,1},{6,2},{7,3},{8,12},{9,13},{10,... | collective-permute-start | bytes 245768 | tf_op jit(solution)/shard_map/ppermute | solution.py:365
  105.6 1.2 collective-permute-done.27
  106.9 1.6 %collective-permute-start.28 = (bf16[64,2304]{1,0:T(8,128)(2,1)S(1)}, bf16[64,2304]{1,0:T(8,128)(2,1)S(1)}, u32[]{:S(2)}, u32[]{:S(2)}) collective-permute-start(bf16[64,2304]{1,0:T(8,128)(2,1)S(1)} %add_convert_fusion), channel_id=1, source_target_pairs={{0,8},{8,0},{16,24},{24,16},{1,9},{9,1},{17,25},{25,17},{2,10},{10... | collective-permute-start | bytes 884744 | tf_op jit(solution)/shard_map/ppermute | solution.py:373
  109.2 2.8 %collective-permute-done.23 = bf16[256,128]{1,0:T(8,128)(2,1)S(1)} collective-permute-done((bf16[256,128]{1,0:T(8,128)(2,1)S(1)}, bf16[256,128]{1,0:T(8,128)(2,1)S(1)}, u32[]{:S(2)}, u32[]{:S(2)}) %collective-permute-start.23) | collective-permute-done | bytes 65568 | tf_op jit(solution)/shard_map/ppermute | solution.py:365
  113.5 1.4 %collective-permute-done.28 = bf16[64,2304]{1,0:T(8,128)(2,1)S(1)} collective-permute-done((bf16[64,2304]{1,0:T(8,128)(2,1)S(1)}, bf16[64,2304]{1,0:T(8,128)(2,1)S(1)}, u32[]{:S(2)}, u32[]{:S(2)}) %collective-permute-start.28) | collective-permute-done | bytes 294944 | tf_op jit(solution)/shard_map/ppermute | solution.py:373
  114.9 1.4 %collective-permute-done.26 = bf16[64,2304]{1,0:T(8,128)(2,1)S(1)} collective-permute-done((bf16[64,2304]{1,0:T(8,128)(2,1)S(1)}, bf16[64,2304]{1,0:T(8,128)(2,1)S(1)}, u32[]{:S(2)}, u32[]{:S(2)}) %collective-permute-start.26) | collective-permute-done | bytes 294944 | tf_op jit(solution)/shard_map/ppermute | solution.py:373
  118.7 1.9 %collective-permute-start.31 = (bf16[192,512]{1,0:T(8,128)(2,1)S(1)}, bf16[192,512]{1,0:T(8,128)(2,1)S(1)}, u32[]{:S(2)}, u32[]{:S(2)}) collective-permute-start(bf16[192,512]{1,0:T(8,128)(2,1)S(1)} %fusion), channel_id=1, source_target_pairs={{0,24},{8,16},{16,8},{24,0},{1,25},{9,17},{17,9},{25,1},{2,26},{10... | collective-permute-start | bytes 589832 | tf_op jit(solution)/shard_map/ppermute | solution.py:380
  122.3 1.5 %collective-permute-done.29 = bf16[192,512]{1,0:T(8,128)(2,1)S(1)} collective-permute-done((bf16[192,512]{1,0:T(8,128)(2,1)S(1)}, bf16[192,512]{1,0:T(8,128)(2,1)S(1)}, u32[]{:S(2)}, u32[]{:S(2)}) %collective-permute-start.29) | collective-permute-done | bytes 196640 | tf_op jit(solution)/shard_map/ppermute | solution.py:380
  123.8 3.0 %collective-permute-done.30 = bf16[192,512]{1,0:T(8,128)(2,1)S(1)} collective-permute-done((bf16[192,512]{1,0:T(8,128)(2,1)S(1)}, bf16[192,512]{1,0:T(8,128)(2,1)S(1)}, u32[]{:S(2)}, u32[]{:S(2)}) %collective-permute-start.30) | collective-permute-done | bytes 196640 | tf_op jit(solution)/shard_map/ppermute | solution.py:380
  (125 shorter events, 15.7 us)
Async XLA Ops:
  0.6 23.8 %collective-permute-start = (bf16[768,512]{1,0:T(8,128)(2,1)}, bf16[768,512]{1,0:T(8,128)(2,1)S(1)}, u32[]{:S(2)}, u32[]{:S(2)}) collective-permute-start(bf16[768,512]{1,0:T(8,128)(2,1)} %refs_2_.1), channel_id=1, source_target_pairs={{2,0},{3,1},{4,2},{5,3},{6,4},{7,5},{10,8},{11,9},{12,10},{13,11},... | collective-permute-start | bytes 2359304 | tf_op jit(solution)/shard_map/ppermute | solution.py:291
  1.9 22.7 %collective-permute-start.1 = (bf16[768,512]{1,0:T(8,128)(2,1)}, bf16[768,512]{1,0:T(8,128)(2,1)}, u32[]{:S(2)}, u32[]{:S(2)}) collective-permute-start(bf16[768,512]{1,0:T(8,128)(2,1)} %refs_2_.1), channel_id=1, source_target_pairs={{0,2},{1,3},{2,4},{3,5},{4,6},{5,7},{8,10},{9,11},{10,12},{11,13},... | collective-permute-start | bytes 2359304 | tf_op jit(solution)/shard_map/ppermute | solution.py:291
  12.3 12.0 %collective-permute-start.2 = (f32[192,384]{1,0:T(8,128)S(1)}, f32[192,384]{1,0:T(8,128)S(1)}, u32[]{:S(2)}, u32[]{:S(2)}) collective-permute-start(f32[192,384]{1,0:T(8,128)S(1)} %slice_select_fusion), channel_id=1, source_target_pairs={{0,1},{1,0},{2,3},{3,2},{4,5},{5,4},{6,7},{7,6},{8,9},{9,8},{10,11... | collective-permute-start | bytes 884744 | tf_op jit(solution)/shard_map/ppermute | solution.py:311
  12.4 20.9 %collective-permute-start.5 = (bf16[768,512]{1,0:T(8,128)(2,1)}, bf16[768,512]{1,0:T(8,128)(2,1)S(1)}, u32[]{:S(2)}, u32[]{:S(2)}) collective-permute-start(bf16[768,512]{1,0:T(8,128)(2,1)} %refs_2_.1), channel_id=1, source_target_pairs={{0,1},{1,0},{2,3},{3,2},{4,5},{5,4},{6,7},{7,6},{8,9},{9,8},{10,11... | collective-permute-start | bytes 2359304 | tf_op jit(solution)/shard_map/ppermute | solution.py:311
  24.7 7.7 %collective-permute-start.9 = (bf16[256,384]{1,0:T(8,128)(2,1)S(1)}, bf16[256,384]{1,0:T(8,128)(2,1)S(1)}, u32[]{:S(2)}, u32[]{:S(2)}) collective-permute-start(bf16[256,384]{1,0:T(8,128)(2,1)S(1)} %pad_maximum_fusion.1), channel_id=1, source_target_pairs={{0,2},{6,4},{1,3},{7,5},{8,10},{14,12},{9,11},{15,13},{16,18},{22,... | collective-permute-start | bytes 589832 | tf_op jit(solution)/shard_map/ppermute | solution.py:350
  29.1 20.0 %collective-permute-start.3 = (bf16[768,512]{1,0:T(8,128)(2,1)S(1)}, bf16[768,512]{1,0:T(8,128)(2,1)S(1)}, u32[]{:S(2)}, u32[]{:S(2)}) collective-permute-start(bf16[768,512]{1,0:T(8,128)(2,1)S(1)} %collective-permute-done), channel_id=1, source_target_pairs={{2,0},{3,1},{4,2},{5,3},{10,8},{11,9},{12,10},{13,11},{18,16},{19,... | collective-permute-start | bytes 2359304 | tf_op jit(solution)/shard_map/ppermute | solution.py:291
  30.4 18.7 %collective-permute-start.4 = (bf16[768,512]{1,0:T(8,128)(2,1)}, bf16[768,512]{1,0:T(8,128)(2,1)S(1)}, u32[]{:S(2)}, u32[]{:S(2)}) collective-permute-start(bf16[768,512]{1,0:T(8,128)(2,1)} %collective-permute-done.1), channel_id=1, source_target_pairs={{2,4},{3,5},{4,6},{5,7},{10,12},{11,13},{12,14},{13,15},{18,20},{1... | collective-permute-start | bytes 2359304 | tf_op jit(solution)/shard_map/ppermute | solution.py:291
  31.2 2.4 %collective-permute-start.6 = (bf16[768,512]{1,0:T(8,128)(2,1)S(1)}, bf16[768,512]{1,0:T(8,128)(2,1)S(1)}, u32[]{:S(2)}, u32[]{:S(2)}) collective-permute-start(bf16[768,512]{1,0:T(8,128)(2,1)S(1)} %broadcast_select_fusion.refs_4_), channel_id=1, source_target_pairs={{0,1},{1,0},{2,3},{3,2},{4,5},{5,4},{6,7},{7,6},{8,9},{9,8},{10,11... | collective-permute-start | bytes 2359304 | tf_op jit(solution)/shard_map/ppermute | solution.py:311
  32.5 16.8 %collective-permute-start.10 = (bf16[256,384]{1,0:T(8,128)(2,1)S(1)}, bf16[256,384]{1,0:T(8,128)(2,1)S(1)}, u32[]{:S(2)}, u32[]{:S(2)}) collective-permute-start(bf16[256,384]{1,0:T(8,128)(2,1)S(1)} %pad_maximum_fusion.2), channel_id=1, source_target_pairs={{2,4},{4,2},{3,5},{5,3},{10,12},{12,10},{11,13},{13,11},{18,20},{2... | collective-permute-start | bytes 589832 | tf_op jit(solution)/shard_map/ppermute | solution.py:350
  49.2 3.3 %collective-permute-start.8 = (bf16[768,512]{1,0:T(8,128)(2,1)S(1)}, bf16[768,512]{1,0:T(8,128)(2,1)S(1)}, u32[]{:S(2)}, u32[]{:S(2)}) collective-permute-start(bf16[768,512]{1,0:T(8,128)(2,1)S(1)} %select_select_fusion.refs_2_), channel_id=1, source_target_pairs={{0,1},{1,0},{2,3},{3,2},{4,5},{5,4},{6,7},{7,6},{8,9},{9,8},{10,11... | collective-permute-start | bytes 2359304 | tf_op jit(solution)/shard_map/ppermute | solution.py:311
  49.6 14.7 %collective-permute-start.13 = (bf16[192,384]{1,0:T(8,128)(2,1)S(1)}, bf16[192,384]{1,0:T(8,128)(2,1)S(1)}, u32[]{:S(2)}, u32[]{:S(2)}) collective-permute-start(bf16[192,384]{1,0:T(8,128)(2,1)S(1)} %fusion.1), channel_id=1, source_target_pairs={{2,0},{4,6},{3,1},{5,7},{10,8},{12,14},{11,9},{13,15},{18,16},{20,... | collective-permute-start | bytes 442376 | tf_op jit(solution)/shard_map/ppermute | solution.py:350
  51.0 13.4 %collective-permute-start.7 = (bf16[256,512]{1,0:T(8,128)(2,1)S(1)}, bf16[256,512]{1,0:T(8,128)(2,1)S(1)}, u32[]{:S(2)}, u32[]{:S(2)}) collective-permute-start(bf16[256,512]{1,0:T(8,128)(2,1)S(1)} %broadcast_select_fusion.2), channel_id=1, source_target_pairs={{2,0},{3,1},{4,6},{5,7},{10,8},{11,9},{12,14},{13,15},{18,16},{19,... | collective-permute-start | bytes 786440 | tf_op jit(solution)/shard_map/ppermute | solution.py:289
  64.4 2.3 %collective-permute-start.14 = (bf16[192,384]{1,0:T(8,128)(2,1)S(1)}, bf16[192,384]{1,0:T(8,128)(2,1)S(1)}, u32[]{:S(2)}, u32[]{:S(2)}) collective-permute-start(bf16[192,384]{1,0:T(8,128)(2,1)S(1)} %broadcast_select_fusion.3), channel_id=1, source_target_pairs={{0,1},{1,0},{2,3},{3,2},{4,5},{5,4},{6,7},{7,6},{8,9},{9,8},{10,11... | collective-permute-start | bytes 442376 | tf_op jit(solution)/shard_map/ppermute | solution.py:311
  64.6 4.4 %collective-permute-start.12 = (bf16[256,512]{1,0:T(8,128)(2,1)S(1)}, bf16[256,512]{1,0:T(8,128)(2,1)S(1)}, u32[]{:S(2)}, u32[]{:S(2)}) collective-permute-start(bf16[256,512]{1,0:T(8,128)(2,1)S(1)} %select_select_fusion.2.refs_2_), channel_id=1, source_target_pairs={{0,1},{1,0},{2,3},{3,2},{4,5},{5,4},{6,7},{7,6},{8,9},{9,8},{10,11... | collective-permute-start | bytes 786440 | tf_op jit(solution)/shard_map/ppermute | solution.py:311
  65.2 15.9 %collective-permute-start.11 = (bf16[512,512]{1,0:T(8,128)(2,1)S(1)}, bf16[512,512]{1,0:T(8,128)(2,1)S(1)}, u32[]{:S(2)}, u32[]{:S(2)}) collective-permute-start(bf16[512,512]{1,0:T(8,128)(2,1)S(1)} %broadcast_select_fusion.1), channel_id=1, source_target_pairs={{2,0},{3,1},{4,6},{5,7},{10,8},{11,9},{12,14},{13,15},{18,16},{19,... | collective-permute-start | bytes 1572872 | tf_op jit(solution)/shard_map/ppermute | solution.py:289
  67.5 9.1 %collective-permute-start.15 = (bf16[64,2304]{1,0:T(8,128)(2,1)S(1)}, bf16[64,2304]{1,0:T(8,128)(2,1)S(1)}, u32[]{:S(2)}, u32[]{:S(2)}) collective-permute-start(bf16[64,2304]{1,0:T(8,128)(2,1)S(1)} %convolution_convert_fusion), channel_id=1, source_target_pairs={{0,8},{8,0},{16,24},{24,16},{1,9},{9,1},{17,25},{25,17},{2,10},{10... | collective-permute-start | bytes 884744 | tf_op jit(solution)/shard_map/ppermute | solution.py:373
  81.1 2.2 %collective-permute-start.17 = (f32[320,128]{1,0:T(8,128)S(1)}, f32[320,128]{1,0:T(8,128)S(1)}, u32[]{:S(2)}, u32[]{:S(2)}) collective-permute-start(f32[320,128]{1,0:T(8,128)S(1)} %fusion.11), channel_id=1, source_target_pairs={{0,1},{1,0},{2,3},{3,2},{4,5},{5,4},{6,7},{7,6},{8,9},{9,8},{10,11... | collective-permute-start | bytes 491528 | tf_op jit(solution)/shard_map/ppermute | solution.py:311
  81.2 2.2 %collective-permute-start.16 = (bf16[512,512]{1,0:T(8,128)(2,1)S(1)}, bf16[512,512]{1,0:T(8,128)(2,1)S(1)}, u32[]{:S(2)}, u32[]{:S(2)}) collective-permute-start(bf16[512,512]{1,0:T(8,128)(2,1)S(1)} %select_select_fusion.1.refs_2_), channel_id=1, source_target_pairs={{0,1},{1,0},{2,3},{3,2},{4,5},{5,4},{6,7},{7,6},{8,9},{9,8},{10,11... | collective-permute-start | bytes 1572872 | tf_op jit(solution)/shard_map/ppermute | solution.py:311
  81.9 12.6 %collective-permute-start.19 = (bf16[64,2304]{1,0:T(8,128)(2,1)S(1)}, bf16[64,2304]{1,0:T(8,128)(2,1)S(1)}, u32[]{:S(2)}, u32[]{:S(2)}) collective-permute-start(bf16[64,2304]{1,0:T(8,128)(2,1)S(1)} %add_convert_fusion.2), channel_id=1, source_target_pairs={{0,16},{8,24},{16,0},{24,8},{1,17},{9,25},{17,1},{25,9},{2,18},{10... | collective-permute-start | bytes 884744 | tf_op jit(solution)/shard_map/ppermute | solution.py:373
  83.3 11.2 %collective-permute-start.18 = (f32[320,128]{1,0:T(8,128)S(1)}, f32[320,128]{1,0:T(8,128)S(1)}, u32[]{:S(2)}, u32[]{:S(2)}) collective-permute-start(f32[320,128]{1,0:T(8,128)S(1)} %select_add_fusion.1), channel_id=1, source_target_pairs={{0,2},{1,3},{2,0},{3,1},{4,6},{5,7},{6,4},{7,5},{8,10},{9,11},{10,... | collective-permute-start | bytes 491528 | tf_op jit(solution)/shard_map/ppermute | solution.py:365
  94.6 1.4 %collective-permute-start.20 = (f32[256,128]{1,0:T(8,128)S(1)}, f32[256,128]{1,0:T(8,128)S(1)}, u32[]{:S(2)}, u32[]{:S(2)}) collective-permute-start(f32[256,128]{1,0:T(8,128)S(1)} %slice_select_fusion.1), channel_id=1, source_target_pairs={{0,1},{1,0},{2,3},{3,2},{4,5},{5,4},{6,7},{7,6},{8,9},{9,8},{10,11... | collective-permute-start | bytes 393224 | tf_op jit(solution)/shard_map/ppermute | solution.py:311
  96.0 5.9 %collective-permute-start.21 = (f32[256,128]{1,0:T(8,128)S(1)}, f32[256,128]{1,0:T(8,128)S(1)}, u32[]{:S(2)}, u32[]{:S(2)}) collective-permute-start(f32[256,128]{1,0:T(8,128)S(1)} %select_add_fusion.2), channel_id=1, source_target_pairs={{0,2},{1,3},{2,0},{3,1},{4,6},{5,7},{6,4},{7,5},{8,10},{9,11},{10,... | collective-permute-start | bytes 393224 | tf_op jit(solution)/shard_map/ppermute | solution.py:365
  98.0 8.8 %collective-permute-start.27 = (bf16[64,2304]{1,0:T(8,128)(2,1)S(1)}, bf16[64,2304]{1,0:T(8,128)(2,1)S(1)}, u32[]{:S(2)}, u32[]{:S(2)}) collective-permute-start(bf16[64,2304]{1,0:T(8,128)(2,1)S(1)} %get-tuple-element.100), channel_id=1, source_target_pairs={{0,16},{8,24},{16,0},{24,8},{1,17},{9,25},{17,1},{25,9},{2,18},{10... | collective-permute-start | bytes 884744 | tf_op jit(solution)/shard_map/ppermute | solution.py:373
  98.7 9.7 %collective-permute-start.25 = (bf16[64,2304]{1,0:T(8,128)(2,1)S(1)}, bf16[64,2304]{1,0:T(8,128)(2,1)S(1)}, u32[]{:S(2)}, u32[]{:S(2)}) collective-permute-start(bf16[64,2304]{1,0:T(8,128)(2,1)S(1)} %get-tuple-element.99), channel_id=1, source_target_pairs={{0,8},{8,0},{16,24},{24,16},{1,9},{9,1},{17,25},{25,17},{2,10},{10... | collective-permute-start | bytes 884744 | tf_op jit(solution)/shard_map/ppermute | solution.py:373
  101.9 10.1 %collective-permute-start.22 = (bf16[320,128]{1,0:T(8,128)(2,1)S(1)}, bf16[320,128]{1,0:T(8,128)(2,1)S(1)}, u32[]{:S(2)}, u32[]{:S(2)}) collective-permute-start(bf16[320,128]{1,0:T(8,128)(2,1)S(1)} %add_convert_fusion.4), channel_id=1, source_target_pairs={{0,4},{1,5},{2,6},{3,7},{4,0},{5,1},{6,2},{7,3},{8,12},{9,13},{10,... | collective-permute-start | bytes 245768 | tf_op jit(solution)/shard_map/ppermute | solution.py:365
  105.5 6.5 %collective-permute-start.23 = (bf16[256,128]{1,0:T(8,128)(2,1)S(1)}, bf16[256,128]{1,0:T(8,128)(2,1)S(1)}, u32[]{:S(2)}, u32[]{:S(2)}) collective-permute-start(bf16[256,128]{1,0:T(8,128)(2,1)S(1)} %add_convert_fusion.6), channel_id=1, source_target_pairs={{0,4},{1,5},{2,6},{3,7},{4,0},{5,1},{6,2},{7,3},{8,12},{9,13},{10,... | collective-permute-start | bytes 196616 | tf_op jit(solution)/shard_map/ppermute | solution.py:365
  106.9 8.0 %collective-permute-start.28 = (bf16[64,2304]{1,0:T(8,128)(2,1)S(1)}, bf16[64,2304]{1,0:T(8,128)(2,1)S(1)}, u32[]{:S(2)}, u32[]{:S(2)}) collective-permute-start(bf16[64,2304]{1,0:T(8,128)(2,1)S(1)} %add_convert_fusion), channel_id=1, source_target_pairs={{0,8},{8,0},{16,24},{24,16},{1,9},{9,1},{17,25},{25,17},{2,10},{10... | collective-permute-start | bytes 884744 | tf_op jit(solution)/shard_map/ppermute | solution.py:373
  108.5 7.7 %collective-permute-start.26 = (bf16[64,2304]{1,0:T(8,128)(2,1)S(1)}, bf16[64,2304]{1,0:T(8,128)(2,1)S(1)}, u32[]{:S(2)}, u32[]{:S(2)}) collective-permute-start(bf16[64,2304]{1,0:T(8,128)(2,1)S(1)} %add_convert_fusion.1), channel_id=1, source_target_pairs={{0,16},{8,24},{16,0},{24,8},{1,17},{9,25},{17,1},{25,9},{2,18},{10... | collective-permute-start | bytes 884744 | tf_op jit(solution)/shard_map/ppermute | solution.py:373
  112.1 1.4 %collective-permute-start.24 = (bf16[576,128]{1,0:T(8,128)(2,1)S(1)}, bf16[576,128]{1,0:T(8,128)(2,1)S(1)}, u32[]{:S(2)}, u32[]{:S(2)}) collective-permute-start(bf16[576,128]{1,0:T(8,128)(2,1)S(1)} %pad_maximum_fusion.5), channel_id=1, source_target_pairs={{0,1},{1,0},{2,3},{3,2},{4,5},{5,4},{6,7},{7,6},{8,9},{9,8},{10,11... | collective-permute-start | bytes 442376 | tf_op jit(solution)/shard_map/ppermute | solution.py:311
  117.0 6.8 %collective-permute-start.29 = (bf16[192,512]{1,0:T(8,128)(2,1)S(1)}, bf16[192,512]{1,0:T(8,128)(2,1)S(1)}, u32[]{:S(2)}, u32[]{:S(2)}) collective-permute-start(bf16[192,512]{1,0:T(8,128)(2,1)S(1)} %fusion), channel_id=1, source_target_pairs={{0,8},{8,0},{16,24},{24,16},{1,9},{9,1},{17,25},{25,17},{2,10},{10... | collective-permute-start | bytes 589832 | tf_op jit(solution)/shard_map/ppermute | solution.py:380
  117.6 9.1 %collective-permute-start.30 = (bf16[192,512]{1,0:T(8,128)(2,1)S(1)}, bf16[192,512]{1,0:T(8,128)(2,1)S(1)}, u32[]{:S(2)}, u32[]{:S(2)}) collective-permute-start(bf16[192,512]{1,0:T(8,128)(2,1)S(1)} %fusion), channel_id=1, source_target_pairs={{0,16},{8,24},{16,0},{24,8},{1,17},{9,25},{17,1},{25,9},{2,18},{10... | collective-permute-start | bytes 589832 | tf_op jit(solution)/shard_map/ppermute | solution.py:380
  118.7 8.1 %collective-permute-start.31 = (bf16[192,512]{1,0:T(8,128)(2,1)S(1)}, bf16[192,512]{1,0:T(8,128)(2,1)S(1)}, u32[]{:S(2)}, u32[]{:S(2)}) collective-permute-start(bf16[192,512]{1,0:T(8,128)(2,1)S(1)} %fusion), channel_id=1, source_target_pairs={{0,24},{8,16},{16,8},{24,0},{1,25},{9,17},{17,9},{25,1},{2,26},{10... | collective-permute-start | bytes 589832 | tf_op jit(solution)/shard_map/ppermute | solution.py:380
  (11 other events, 125.1 us)

commit v3 on v2

--- a/solution.py
+++ b/solution.py
@@ -487,12 +487,13 @@
     across = places.send_across(after, 1)
     k = 2
     while k < places.chips:
-        before, across = barrier((before, across))
+        before, across, sent = barrier((before, across, sent))
+        if k == 2:
+            large = [summed(pair) for pair in sent]
+            sent = [places.dp_send(x, order[1]) for x, order in zip(large, bits)]
         before = places.send_across(summed(before), k)
         across = places.send_across(summed(across), k)
         k *= 2
-    large = [summed(pair) for pair in sent]
-    sent = [places.dp_send(x, order[1]) for x, order in zip(large, bits)]
     total = jnp.concatenate([summed(before), summed(across)], axis=0).astype(BF)
     other, sent = barrier((places.swap(total), sent))
     large = [summed(pair) for pair in sent]

time: 128 us -> 133 us (1.039)
  waiting for transfers between devices: 29.8 us -> 35.7 us
    ppermute x4, waiting for transfers between devices: 4.53 us -> 10.3 us  [send_across(): return (mine, lax.ppermute(mine, 'tensor', pairs))]
    ppermute x3, waiting for transfers between devices: 4.44 us -> 7.06 us  [sum_four(): gots.append(lax.ppermute(mine, 'dp', pairs))]
    ppermute x6, waiting for transfers between devices: 4.31 us -> 2.84 us  [dp_send(): lax.ppermute(mine, 'dp', [(i, i ^ bit) for i in range(self.dps)])]
  transfers between devices with their start and end apart: 32 -> 32, of which waited for: 16 -> 15; matrix products, arithmetic and copies ran while one was open for 5% -> 4% of each run, Pallas kernels for 40% -> 38%
where the time goes in v3:
time: 133 us
  Pallas kernels  50.8 us (38%)
  starting transfers between devices  37.3 us (28%)
  waiting for transfers between devices  35.7 us (27%)
  other arithmetic  5.13 us (4%)
  between operations  1.38 us (1%)
    pallas_call x4, Pallas kernels, grad_call(): pl.pallas_call(functools.partial(grad_kernel, len(blocks), acc is not Non...  36.5 us
    pallas_call x1, Pallas kernels, hidden_call(): pl.pallas_call(hidden_kernel, grid=(hidden // tile,), in_specs=[wide, wid...  11.4 us
    ppermute x4, waiting for transfers between devices, send_across(): return (mine, lax.ppermute(mine, 'tensor', pairs))  10.3 us
    ppermute x2, waiting for transfers between devices, flood(): both = lax.ppermute(chosen, 'tensor', pairs[0] + pairs[1])  9.16 us
    ppermute x6, starting transfers between devices, dp_send(): lax.ppermute(mine, 'dp', [(i, i ^ bit) for i in range(self.dps)])  7.58 us
    ppermute x2, starting transfers between devices, flood(): lax.ppermute(down, 'tensor', pairs[1])  7.16 us
    ppermute x3, waiting for transfers between devices, sum_four(): gots.append(lax.ppermute(mine, 'dp', pairs))  7.06 us
    ppermute x3, starting transfers between devices, low_send(): return (mine, lax.ppermute(mine, 'tensor', pairs))  6.49 us
  transfers between devices with their start and end apart: 32, of which 15 were waited for; matrix products, arithmetic and copies ran while one was open for 4% of the time, Pallas kernels for 38%

profile of v3, /device:TPU:0, one launch (start us, length us, event | category | flops | bytes accessed | tf_op | source)
XLA Modules:
  0.0 132.6 jit_solution(310976575823000255)
XLA Ops:
  0.6 1.3 collective-permute-start
  1.9 6.4 %collective-permute-start.1 = (bf16[768,512]{1,0:T(8,128)(2,1)}, bf16[768,512]{1,0:T(8,128)(2,1)}, u32[]{:S(2)}, u32[]{:S(2)}) collective-permute-start(bf16[768,512]{1,0:T(8,128)(2,1)} %refs_2_.1), channel_id=1, source_target_pairs={{0,2},{1,3},{2,4},{3,5},{4,6},{5,7},{8,10},{9,11},{10,12},{11,13},... | collective-permute-start | bytes 2359304 | tf_op jit(solution)/shard_map/ppermute | solution.py:291
  8.4 2.9 %low.1 = f32[192,768]{1,0:T(8,128)} custom-call(bf16[768,512]{1,0:T(8,128)(2,1)} %x_ref, bf16[64,512]{1,0:T(8,128)(2,1)} %bitcast.20, bf16[64,512]{1,0:T(8,128)(2,1)} %bitcast.21, bf16[768,512]{1,0:T(8,128)(2,1)} %refs_2_.1, bf16[64,512]{1,0:T(8,128)(2,1)} %s_ref.1), custom_call_target="tpu_custom_call" | custom-call | flops 1024 | bytes 1024 | tf_op jit(solution)/shard_map/low/pallas_call | solution.py:171
  12.9 11.4 %hidden.1 = (f32[384,128]{1,0:T(8,128)}, bf16[768,2304]{1,0:T(8,128)(2,1)}, f32[768,2304]{1,0:T(8,128)}, f32[768,2304]{1,0:T(8,128)}) custom-call(bf16[768,2304]{1,0:T(8,128)(2,1)} %gate_ref.1, bf16[768,2304]{1,0:T(8,128)(2,1)} %up_ref.1, bf16[64,2304]{1,0:T(8,128)(2,1)} %bitcast.17), custom_call_target="tpu_custom_call" | custom-call | flops 1024 | bytes 1024 | tf_op jit(solution)/shard_map/hidden/pallas_call | solution.py:212
  24.7 4.4 %collective-permute-start.9 = (bf16[256,384]{1,0:T(8,128)(2,1)S(1)}, bf16[256,384]{1,0:T(8,128)(2,1)S(1)}, u32[]{:S(2)}, u32[]{:S(2)}) collective-permute-start(bf16[256,384]{1,0:T(8,128)(2,1)S(1)} %pad_maximum_fusion.1), channel_id=1, source_target_pairs={{0,2},{6,4},{1,3},{7,5},{8,10},{14,12},{9,11},{15,13},{16,18},{22,... | collective-permute-start | bytes 589832 | tf_op jit(solution)/shard_map/ppermute | solution.py:350
  29.1 1.3 collective-permute-start.3
  33.6 11.2 %more.2.refs_6_ = f32[768,2304]{1,0:T(8,128)S(1)} custom-call(s32[64]{0:T(128)S(1)} %copy-done.4, s32[1]{0:T(128)} %bitcast.refs_1_, bf16[768,512]{1,0:T(8,128)(2,1)S(1)} %copy-done, bf16[768,512]{1,0:T(8,128)(2,1)S(1)} %collective-permute-done.5.refs_3_, bf16[768,512]{1,0:T(8,128)(2,1)S(1)} %broadcast_select_fusion.refs_4_, ...), custom_call_target="tpu_custom_call" | custom-call | flops 7247757312 | bytes 23592960 | tf_op jit(solution)/shard_map/more/pallas_call | solution.py:145
  44.7 4.4 %collective-permute-done.3 = bf16[768,512]{1,0:T(8,128)(2,1)S(1)} collective-permute-done((bf16[768,512]{1,0:T(8,128)(2,1)S(1)}, bf16[768,512]{1,0:T(8,128)(2,1)S(1)}, u32[]{:S(2)}, u32[]{:S(2)}) %collective-permute-start.3) | collective-permute-done | bytes 786464 | tf_op jit(solution)/shard_map/ppermute | solution.py:291
  49.6 1.3 collective-permute-start.13
  51.0 1.6 %collective-permute-start.7 = (bf16[256,512]{1,0:T(8,128)(2,1)S(1)}, bf16[256,512]{1,0:T(8,128)(2,1)S(1)}, u32[]{:S(2)}, u32[]{:S(2)}) collective-permute-start(bf16[256,512]{1,0:T(8,128)(2,1)S(1)} %broadcast_select_fusion.2), channel_id=1, source_target_pairs={{2,0},{3,1},{4,6},{5,7},{10,8},{11,9},{12,14},{13,15},{18,16},{19,... | collective-permute-start | bytes 786440 | tf_op jit(solution)/shard_map/ppermute | solution.py:289
  52.6 7.1 %more.3.refs_6_ = f32[768,2304]{1,0:T(8,128)S(1)} custom-call(s32[64]{0:T(128)S(1)} %copy-done.4, s32[1]{0:T(128)} %bitcast.refs_1_, bf16[768,512]{1,0:T(8,128)(2,1)S(1)} %select_select_fusion.refs_2_, bf16[768,512]{1,0:T(8,128)(2,1)S(1)} %collective-permute-done.8.refs_3_, bf16[2304,4096]{1,0:T(8,128)(2,1)} %refs_5_.5, bf16[2304,4096]{1,0:T(8,128)(2,1)} %refs_5_.5, ...), custom_call_target="tpu_custom_call" | custom-call | flops 3623878656 | bytes 18874368 | tf_op jit(solution)/shard_map/more/pallas_call | solution.py:145
  59.6 4.7 %collective-permute-done.7 = bf16[256,512]{1,0:T(8,128)(2,1)S(1)} collective-permute-done((bf16[256,512]{1,0:T(8,128)(2,1)S(1)}, bf16[256,512]{1,0:T(8,128)(2,1)S(1)}, u32[]{:S(2)}, u32[]{:S(2)}) %collective-permute-start.7) | collective-permute-done | bytes 262176 | tf_op jit(solution)/shard_map/ppermute | solution.py:289
  65.2 1.5 %collective-permute-start.11 = (bf16[512,512]{1,0:T(8,128)(2,1)S(1)}, bf16[512,512]{1,0:T(8,128)(2,1)S(1)}, u32[]{:S(2)}, u32[]{:S(2)}) collective-permute-start(bf16[512,512]{1,0:T(8,128)(2,1)S(1)} %broadcast_select_fusion.1), channel_id=1, source_target_pairs={{2,0},{3,1},{4,6},{5,7},{10,8},{11,9},{12,14},{13,15},{18,16},{19,... | collective-permute-start | bytes 1572872 | tf_op jit(solution)/shard_map/ppermute | solution.py:289
  67.5 1.4 %collective-permute-start.15 = (bf16[64,2304]{1,0:T(8,128)(2,1)S(1)}, bf16[64,2304]{1,0:T(8,128)(2,1)S(1)}, u32[]{:S(2)}, u32[]{:S(2)}) collective-permute-start(bf16[64,2304]{1,0:T(8,128)(2,1)S(1)} %convolution_convert_fusion), channel_id=1, source_target_pairs={{0,8},{8,0},{16,24},{24,16},{1,9},{9,1},{17,25},{25,17},{2,10},{10... | collective-permute-start | bytes 884744 | tf_op jit(solution)/shard_map/ppermute | solution.py:373
  69.0 7.3 %last_a.1 = (f32[256,128]{1,0:T(8,128)S(1)}, f32[128,2304]{1,0:T(8,128)S(1)}) custom-call(s32[64]{0:T(128)S(1)} %copy-done.4, s32[1]{0:T(128)} %bitcast.refs_1_, bf16[256,512]{1,0:T(8,128)(2,1)S(1)} %select_select_fusion.2.refs_2_, bf16[256,512]{1,0:T(8,128)(2,1)S(1)} %collective-permute-done.12.refs_3_, bf16[2304,4096]{1,0:T(8,128)(2,1)} %refs_5_.5, ...), custom_call_target="tpu_custom_call" | custom-call | flops 2415919104 | bytes 9437184 | tf_op jit(solution)/shard_map/last_a/pallas_call | solution.py:145
  76.6 4.4 %collective-permute-done.11 = bf16[512,512]{1,0:T(8,128)(2,1)S(1)} collective-permute-done((bf16[512,512]{1,0:T(8,128)(2,1)S(1)}, bf16[512,512]{1,0:T(8,128)(2,1)S(1)}, u32[]{:S(2)}, u32[]{:S(2)}) %collective-permute-start.11) | collective-permute-done | bytes 524320 | tf_op jit(solution)/shard_map/ppermute | solution.py:289
  81.9 1.4 %collective-permute-start.19 = (bf16[64,2304]{1,0:T(8,128)(2,1)S(1)}, bf16[64,2304]{1,0:T(8,128)(2,1)S(1)}, u32[]{:S(2)}, u32[]{:S(2)}) collective-permute-start(bf16[64,2304]{1,0:T(8,128)(2,1)S(1)} %add_convert_fusion.2), channel_id=1, source_target_pairs={{0,16},{8,24},{16,0},{24,8},{1,17},{9,25},{17,1},{25,9},{2,18},{10... | collective-permute-start | bytes 884744 | tf_op jit(solution)/shard_map/ppermute | solution.py:373
  83.4 11.1 %last_b.1 = (f32[512,128]{1,0:T(8,128)S(1)}, bf16[64,2304]{1,0:T(8,128)(2,1)S(1)}, bf16[64,2304]{1,0:T(8,128)(2,1)S(1)}) custom-call(s32[64]{0:T(128)S(1)} %copy-done.4, s32[1]{0:T(128)} %bitcast.refs_1_, bf16[512,512]{1,0:T(8,128)(2,1)S(1)} %select_select_fusion.1.refs_2_, bf16[512,512]{1,0:T(8,128)(2,1)S(1)} %collective-permute-done.16.refs_3_, ...), custom_call_target="tpu_custom_call" | custom-call | flops 4831838208 | bytes 14155776 | tf_op jit(solution)/shard_map/last_b/pallas_call | solution.py:145
  94.9 1.3 %collective-permute-start.22 = (bf16[64,2304]{1,0:T(8,128)(2,1)S(1)}, bf16[64,2304]{1,0:T(8,128)(2,1)S(1)}, u32[]{:S(2)}, u32[]{:S(2)}) collective-permute-start(bf16[64,2304]{1,0:T(8,128)(2,1)S(1)} %get-tuple-element.105), channel_id=1, source_target_pairs={{0,8},{8,0},{16,24},{24,16},{1,9},{9,1},{17,25},{25,17},{2,10},{10... | collective-permute-start | bytes 884744 | tf_op jit(solution)/shard_map/ppermute | solution.py:373
  96.2 1.5 %collective-permute-start.23 = (bf16[64,2304]{1,0:T(8,128)(2,1)S(1)}, bf16[64,2304]{1,0:T(8,128)(2,1)S(1)}, u32[]{:S(2)}, u32[]{:S(2)}) collective-permute-start(bf16[64,2304]{1,0:T(8,128)(2,1)S(1)} %get-tuple-element.107), channel_id=1, source_target_pairs={{0,16},{8,24},{16,0},{24,8},{1,17},{9,25},{17,1},{25,9},{2,18},{10... | collective-permute-start | bytes 884744 | tf_op jit(solution)/shard_map/ppermute | solution.py:373
  97.8 1.1 collective-permute-start.21
  98.9 3.9 %collective-permute-done.21 = f32[256,128]{1,0:T(8,128)S(1)} collective-permute-done((f32[256,128]{1,0:T(8,128)S(1)}, f32[256,128]{1,0:T(8,128)S(1)}, u32[]{:S(2)}, u32[]{:S(2)}) %collective-permute-start.21) | collective-permute-done | bytes 131104 | tf_op jit(solution)/shard_map/ppermute | solution.py:365
  102.8 1.2 collective-permute-done.22
  104.0 1.2 collective-permute-done.23
  106.0 1.3 %collective-permute-start.27 = (bf16[64,2304]{1,0:T(8,128)(2,1)S(1)}, bf16[64,2304]{1,0:T(8,128)(2,1)S(1)}, u32[]{:S(2)}, u32[]{:S(2)}) collective-permute-start(bf16[64,2304]{1,0:T(8,128)(2,1)S(1)} %add_convert_fusion.1), channel_id=1, source_target_pairs={{0,16},{8,24},{16,0},{24,8},{1,17},{9,25},{17,1},{25,9},{2,18},{10... | collective-permute-start | bytes 884744 | tf_op jit(solution)/shard_map/ppermute | solution.py:373
  107.3 3.3 %collective-permute-start.25 = (bf16[256,128]{1,0:T(8,128)(2,1)S(1)}, bf16[256,128]{1,0:T(8,128)(2,1)S(1)}, u32[]{:S(2)}, u32[]{:S(2)}) collective-permute-start(bf16[256,128]{1,0:T(8,128)(2,1)S(1)} %add_convert_fusion.6), channel_id=1, source_target_pairs={{0,4},{1,5},{2,6},{3,7},{4,0},{5,1},{6,2},{7,3},{8,12},{9,13},{10,... | collective-permute-start | bytes 196616 | tf_op jit(solution)/shard_map/ppermute | solution.py:365
  110.7 4.1 %collective-permute-done.25 = bf16[256,128]{1,0:T(8,128)(2,1)S(1)} collective-permute-done((bf16[256,128]{1,0:T(8,128)(2,1)S(1)}, bf16[256,128]{1,0:T(8,128)(2,1)S(1)}, u32[]{:S(2)}, u32[]{:S(2)}) %collective-permute-start.25) | collective-permute-done | bytes 65568 | tf_op jit(solution)/shard_map/ppermute | solution.py:365
  114.9 2.2 %collective-permute-done.24 = bf16[320,128]{1,0:T(8,128)(2,1)S(1)} collective-permute-done((bf16[320,128]{1,0:T(8,128)(2,1)S(1)}, bf16[320,128]{1,0:T(8,128)(2,1)S(1)}, u32[]{:S(2)}, u32[]{:S(2)}) %collective-permute-start.24) | collective-permute-done | bytes 81952 | tf_op jit(solution)/shard_map/ppermute | solution.py:365
  119.4 1.5 %collective-permute-start.29 = (bf16[192,512]{1,0:T(8,128)(2,1)S(1)}, bf16[192,512]{1,0:T(8,128)(2,1)S(1)}, u32[]{:S(2)}, u32[]{:S(2)}) collective-permute-start(bf16[192,512]{1,0:T(8,128)(2,1)S(1)} %fusion), channel_id=1, source_target_pairs={{0,8},{8,0},{16,24},{24,16},{1,9},{9,1},{17,25},{25,17},{2,10},{10... | collective-permute-start | bytes 589832 | tf_op jit(solution)/shard_map/ppermute | solution.py:380
  120.9 1.4 %collective-permute-start.30 = (bf16[192,512]{1,0:T(8,128)(2,1)S(1)}, bf16[192,512]{1,0:T(8,128)(2,1)S(1)}, u32[]{:S(2)}, u32[]{:S(2)}) collective-permute-start(bf16[192,512]{1,0:T(8,128)(2,1)S(1)} %fusion), channel_id=1, source_target_pairs={{0,16},{8,24},{16,0},{24,8},{1,17},{9,25},{17,1},{25,9},{2,18},{10... | collective-permute-start | bytes 589832 | tf_op jit(solution)/shard_map/ppermute | solution.py:380
  124.7 2.5 %collective-permute-done.29 = bf16[192,512]{1,0:T(8,128)(2,1)S(1)} collective-permute-done((bf16[192,512]{1,0:T(8,128)(2,1)S(1)}, bf16[192,512]{1,0:T(8,128)(2,1)S(1)}, u32[]{:S(2)}, u32[]{:S(2)}) %collective-permute-start.29) | collective-permute-done | bytes 196640 | tf_op jit(solution)/shard_map/ppermute | solution.py:380
  127.2 4.6 %collective-permute-done.30 = bf16[192,512]{1,0:T(8,128)(2,1)S(1)} collective-permute-done((bf16[192,512]{1,0:T(8,128)(2,1)S(1)}, bf16[192,512]{1,0:T(8,128)(2,1)S(1)}, u32[]{:S(2)}, u32[]{:S(2)}) %collective-permute-start.30) | collective-permute-done | bytes 196640 | tf_op jit(solution)/shard_map/ppermute | solution.py:380
  (125 shorter events, 15.0 us)
Async XLA Ops:
  0.6 23.8 %collective-permute-start = (bf16[768,512]{1,0:T(8,128)(2,1)}, bf16[768,512]{1,0:T(8,128)(2,1)S(1)}, u32[]{:S(2)}, u32[]{:S(2)}) collective-permute-start(bf16[768,512]{1,0:T(8,128)(2,1)} %refs_2_.1), channel_id=1, source_target_pairs={{2,0},{3,1},{4,2},{5,3},{6,4},{7,5},{10,8},{11,9},{12,10},{13,11},... | collective-permute-start | bytes 2359304 | tf_op jit(solution)/shard_map/ppermute | solution.py:291
  1.9 22.7 %collective-permute-start.1 = (bf16[768,512]{1,0:T(8,128)(2,1)}, bf16[768,512]{1,0:T(8,128)(2,1)}, u32[]{:S(2)}, u32[]{:S(2)}) collective-permute-start(bf16[768,512]{1,0:T(8,128)(2,1)} %refs_2_.1), channel_id=1, source_target_pairs={{0,2},{1,3},{2,4},{3,5},{4,6},{5,7},{8,10},{9,11},{10,12},{11,13},... | collective-permute-start | bytes 2359304 | tf_op jit(solution)/shard_map/ppermute | solution.py:291
  12.3 12.0 %collective-permute-start.2 = (f32[192,384]{1,0:T(8,128)S(1)}, f32[192,384]{1,0:T(8,128)S(1)}, u32[]{:S(2)}, u32[]{:S(2)}) collective-permute-start(f32[192,384]{1,0:T(8,128)S(1)} %slice_select_fusion), channel_id=1, source_target_pairs={{0,1},{1,0},{2,3},{3,2},{4,5},{5,4},{6,7},{7,6},{8,9},{9,8},{10,11... | collective-permute-start | bytes 884744 | tf_op jit(solution)/shard_map/ppermute | solution.py:311
  12.4 20.9 %collective-permute-start.5 = (bf16[768,512]{1,0:T(8,128)(2,1)}, bf16[768,512]{1,0:T(8,128)(2,1)S(1)}, u32[]{:S(2)}, u32[]{:S(2)}) collective-permute-start(bf16[768,512]{1,0:T(8,128)(2,1)} %refs_2_.1), channel_id=1, source_target_pairs={{0,1},{1,0},{2,3},{3,2},{4,5},{5,4},{6,7},{7,6},{8,9},{9,8},{10,11... | collective-permute-start | bytes 2359304 | tf_op jit(solution)/shard_map/ppermute | solution.py:311
  24.7 7.7 %collective-permute-start.9 = (bf16[256,384]{1,0:T(8,128)(2,1)S(1)}, bf16[256,384]{1,0:T(8,128)(2,1)S(1)}, u32[]{:S(2)}, u32[]{:S(2)}) collective-permute-start(bf16[256,384]{1,0:T(8,128)(2,1)S(1)} %pad_maximum_fusion.1), channel_id=1, source_target_pairs={{0,2},{6,4},{1,3},{7,5},{8,10},{14,12},{9,11},{15,13},{16,18},{22,... | collective-permute-start | bytes 589832 | tf_op jit(solution)/shard_map/ppermute | solution.py:350
  29.1 20.0 %collective-permute-start.3 = (bf16[768,512]{1,0:T(8,128)(2,1)S(1)}, bf16[768,512]{1,0:T(8,128)(2,1)S(1)}, u32[]{:S(2)}, u32[]{:S(2)}) collective-permute-start(bf16[768,512]{1,0:T(8,128)(2,1)S(1)} %collective-permute-done), channel_id=1, source_target_pairs={{2,0},{3,1},{4,2},{5,3},{10,8},{11,9},{12,10},{13,11},{18,16},{19,... | collective-permute-start | bytes 2359304 | tf_op jit(solution)/shard_map/ppermute | solution.py:291
  30.4 18.7 %collective-permute-start.4 = (bf16[768,512]{1,0:T(8,128)(2,1)}, bf16[768,512]{1,0:T(8,128)(2,1)S(1)}, u32[]{:S(2)}, u32[]{:S(2)}) collective-permute-start(bf16[768,512]{1,0:T(8,128)(2,1)} %collective-permute-done.1), channel_id=1, source_target_pairs={{2,4},{3,5},{4,6},{5,7},{10,12},{11,13},{12,14},{13,15},{18,20},{1... | collective-permute-start | bytes 2359304 | tf_op jit(solution)/shard_map/ppermute | solution.py:291
  31.2 2.4 %collective-permute-start.6 = (bf16[768,512]{1,0:T(8,128)(2,1)S(1)}, bf16[768,512]{1,0:T(8,128)(2,1)S(1)}, u32[]{:S(2)}, u32[]{:S(2)}) collective-permute-start(bf16[768,512]{1,0:T(8,128)(2,1)S(1)} %broadcast_select_fusion.refs_4_), channel_id=1, source_target_pairs={{0,1},{1,0},{2,3},{3,2},{4,5},{5,4},{6,7},{7,6},{8,9},{9,8},{10,11... | collective-permute-start | bytes 2359304 | tf_op jit(solution)/shard_map/ppermute | solution.py:311
  32.5 16.8 %collective-permute-start.10 = (bf16[256,384]{1,0:T(8,128)(2,1)S(1)}, bf16[256,384]{1,0:T(8,128)(2,1)S(1)}, u32[]{:S(2)}, u32[]{:S(2)}) collective-permute-start(bf16[256,384]{1,0:T(8,128)(2,1)S(1)} %pad_maximum_fusion.2), channel_id=1, source_target_pairs={{2,4},{4,2},{3,5},{5,3},{10,12},{12,10},{11,13},{13,11},{18,20},{2... | collective-permute-start | bytes 589832 | tf_op jit(solution)/shard_map/ppermute | solution.py:350
  49.2 3.3 %collective-permute-start.8 = (bf16[768,512]{1,0:T(8,128)(2,1)S(1)}, bf16[768,512]{1,0:T(8,128)(2,1)S(1)}, u32[]{:S(2)}, u32[]{:S(2)}) collective-permute-start(bf16[768,512]{1,0:T(8,128)(2,1)S(1)} %select_select_fusion.refs_2_), channel_id=1, source_target_pairs={{0,1},{1,0},{2,3},{3,2},{4,5},{5,4},{6,7},{7,6},{8,9},{9,8},{10,11... | collective-permute-start | bytes 2359304 | tf_op jit(solution)/shard_map/ppermute | solution.py:311
  49.6 14.7 %collective-permute-start.13 = (bf16[192,384]{1,0:T(8,128)(2,1)S(1)}, bf16[192,384]{1,0:T(8,128)(2,1)S(1)}, u32[]{:S(2)}, u32[]{:S(2)}) collective-permute-start(bf16[192,384]{1,0:T(8,128)(2,1)S(1)} %fusion.1), channel_id=1, source_target_pairs={{2,0},{4,6},{3,1},{5,7},{10,8},{12,14},{11,9},{13,15},{18,16},{20,... | collective-permute-start | bytes 442376 | tf_op jit(solution)/shard_map/ppermute | solution.py:350
  51.0 13.4 %collective-permute-start.7 = (bf16[256,512]{1,0:T(8,128)(2,1)S(1)}, bf16[256,512]{1,0:T(8,128)(2,1)S(1)}, u32[]{:S(2)}, u32[]{:S(2)}) collective-permute-start(bf16[256,512]{1,0:T(8,128)(2,1)S(1)} %broadcast_select_fusion.2), channel_id=1, source_target_pairs={{2,0},{3,1},{4,6},{5,7},{10,8},{11,9},{12,14},{13,15},{18,16},{19,... | collective-permute-start | bytes 786440 | tf_op jit(solution)/shard_map/ppermute | solution.py:289
  64.4 2.3 %collective-permute-start.14 = (bf16[192,384]{1,0:T(8,128)(2,1)S(1)}, bf16[192,384]{1,0:T(8,128)(2,1)S(1)}, u32[]{:S(2)}, u32[]{:S(2)}) collective-permute-start(bf16[192,384]{1,0:T(8,128)(2,1)S(1)} %broadcast_select_fusion.3), channel_id=1, source_target_pairs={{0,1},{1,0},{2,3},{3,2},{4,5},{5,4},{6,7},{7,6},{8,9},{9,8},{10,11... | collective-permute-start | bytes 442376 | tf_op jit(solution)/shard_map/ppermute | solution.py:311
  64.6 4.4 %collective-permute-start.12 = (bf16[256,512]{1,0:T(8,128)(2,1)S(1)}, bf16[256,512]{1,0:T(8,128)(2,1)S(1)}, u32[]{:S(2)}, u32[]{:S(2)}) collective-permute-start(bf16[256,512]{1,0:T(8,128)(2,1)S(1)} %select_select_fusion.2.refs_2_), channel_id=1, source_target_pairs={{0,1},{1,0},{2,3},{3,2},{4,5},{5,4},{6,7},{7,6},{8,9},{9,8},{10,11... | collective-permute-start | bytes 786440 | tf_op jit(solution)/shard_map/ppermute | solution.py:311
  65.2 15.9 %collective-permute-start.11 = (bf16[512,512]{1,0:T(8,128)(2,1)S(1)}, bf16[512,512]{1,0:T(8,128)(2,1)S(1)}, u32[]{:S(2)}, u32[]{:S(2)}) collective-permute-start(bf16[512,512]{1,0:T(8,128)(2,1)S(1)} %broadcast_select_fusion.1), channel_id=1, source_target_pairs={{2,0},{3,1},{4,6},{5,7},{10,8},{11,9},{12,14},{13,15},{18,16},{19,... | collective-permute-start | bytes 1572872 | tf_op jit(solution)/shard_map/ppermute | solution.py:289
  67.5 9.1 %collective-permute-start.15 = (bf16[64,2304]{1,0:T(8,128)(2,1)S(1)}, bf16[64,2304]{1,0:T(8,128)(2,1)S(1)}, u32[]{:S(2)}, u32[]{:S(2)}) collective-permute-start(bf16[64,2304]{1,0:T(8,128)(2,1)S(1)} %convolution_convert_fusion), channel_id=1, source_target_pairs={{0,8},{8,0},{16,24},{24,16},{1,9},{9,1},{17,25},{25,17},{2,10},{10... | collective-permute-start | bytes 884744 | tf_op jit(solution)/shard_map/ppermute | solution.py:373
  81.1 2.2 %collective-permute-start.17 = (f32[320,128]{1,0:T(8,128)S(1)}, f32[320,128]{1,0:T(8,128)S(1)}, u32[]{:S(2)}, u32[]{:S(2)}) collective-permute-start(f32[320,128]{1,0:T(8,128)S(1)} %fusion.11), channel_id=1, source_target_pairs={{0,1},{1,0},{2,3},{3,2},{4,5},{5,4},{6,7},{7,6},{8,9},{9,8},{10,11... | collective-permute-start | bytes 491528 | tf_op jit(solution)/shard_map/ppermute | solution.py:311
  81.2 2.2 %collective-permute-start.16 = (bf16[512,512]{1,0:T(8,128)(2,1)S(1)}, bf16[512,512]{1,0:T(8,128)(2,1)S(1)}, u32[]{:S(2)}, u32[]{:S(2)}) collective-permute-start(bf16[512,512]{1,0:T(8,128)(2,1)S(1)} %select_select_fusion.1.refs_2_), channel_id=1, source_target_pairs={{0,1},{1,0},{2,3},{3,2},{4,5},{5,4},{6,7},{7,6},{8,9},{9,8},{10,11... | collective-permute-start | bytes 1572872 | tf_op jit(solution)/shard_map/ppermute | solution.py:311
  81.9 12.6 %collective-permute-start.19 = (bf16[64,2304]{1,0:T(8,128)(2,1)S(1)}, bf16[64,2304]{1,0:T(8,128)(2,1)S(1)}, u32[]{:S(2)}, u32[]{:S(2)}) collective-permute-start(bf16[64,2304]{1,0:T(8,128)(2,1)S(1)} %add_convert_fusion.2), channel_id=1, source_target_pairs={{0,16},{8,24},{16,0},{24,8},{1,17},{9,25},{17,1},{25,9},{2,18},{10... | collective-permute-start | bytes 884744 | tf_op jit(solution)/shard_map/ppermute | solution.py:373
  83.3 11.2 %collective-permute-start.18 = (f32[320,128]{1,0:T(8,128)S(1)}, f32[320,128]{1,0:T(8,128)S(1)}, u32[]{:S(2)}, u32[]{:S(2)}) collective-permute-start(f32[320,128]{1,0:T(8,128)S(1)} %select_add_fusion.1), channel_id=1, source_target_pairs={{0,2},{1,3},{2,0},{3,1},{4,6},{5,7},{6,4},{7,5},{8,10},{9,11},{10,... | collective-permute-start | bytes 491528 | tf_op jit(solution)/shard_map/ppermute | solution.py:365
  94.5 3.2 %collective-permute-start.20 = (f32[256,128]{1,0:T(8,128)S(1)}, f32[256,128]{1,0:T(8,128)S(1)}, u32[]{:S(2)}, u32[]{:S(2)}) collective-permute-start(f32[256,128]{1,0:T(8,128)S(1)} %slice_select_fusion.1), channel_id=1, source_target_pairs={{0,1},{1,0},{2,3},{3,2},{4,5},{5,4},{6,7},{7,6},{8,9},{9,8},{10,11... | collective-permute-start | bytes 393224 | tf_op jit(solution)/shard_map/ppermute | solution.py:311
  94.9 9.2 %collective-permute-start.22 = (bf16[64,2304]{1,0:T(8,128)(2,1)S(1)}, bf16[64,2304]{1,0:T(8,128)(2,1)S(1)}, u32[]{:S(2)}, u32[]{:S(2)}) collective-permute-start(bf16[64,2304]{1,0:T(8,128)(2,1)S(1)} %get-tuple-element.105), channel_id=1, source_target_pairs={{0,8},{8,0},{16,24},{24,16},{1,9},{9,1},{17,25},{25,17},{2,10},{10... | collective-permute-start | bytes 884744 | tf_op jit(solution)/shard_map/ppermute | solution.py:373
  96.2 9.1 %collective-permute-start.23 = (bf16[64,2304]{1,0:T(8,128)(2,1)S(1)}, bf16[64,2304]{1,0:T(8,128)(2,1)S(1)}, u32[]{:S(2)}, u32[]{:S(2)}) collective-permute-start(bf16[64,2304]{1,0:T(8,128)(2,1)S(1)} %get-tuple-element.107), channel_id=1, source_target_pairs={{0,16},{8,24},{16,0},{24,8},{1,17},{9,25},{17,1},{25,9},{2,18},{10... | collective-permute-start | bytes 884744 | tf_op jit(solution)/shard_map/ppermute | solution.py:373
  97.8 5.0 %collective-permute-start.21 = (f32[256,128]{1,0:T(8,128)S(1)}, f32[256,128]{1,0:T(8,128)S(1)}, u32[]{:S(2)}, u32[]{:S(2)}) collective-permute-start(f32[256,128]{1,0:T(8,128)S(1)} %select_add_fusion.2), channel_id=1, source_target_pairs={{0,2},{1,3},{2,0},{3,1},{4,6},{5,7},{6,4},{7,5},{8,10},{9,11},{10,... | collective-permute-start | bytes 393224 | tf_op jit(solution)/shard_map/ppermute | solution.py:365
  105.3 13.2 %collective-permute-start.28 = (bf16[64,2304]{1,0:T(8,128)(2,1)S(1)}, bf16[64,2304]{1,0:T(8,128)(2,1)S(1)}, u32[]{:S(2)}, u32[]{:S(2)}) collective-permute-start(bf16[64,2304]{1,0:T(8,128)(2,1)S(1)} %add_convert_fusion), channel_id=1, source_target_pairs={{0,8},{8,0},{16,24},{24,16},{1,9},{9,1},{17,25},{25,17},{2,10},{10... | collective-permute-start | bytes 884744 | tf_op jit(solution)/shard_map/ppermute | solution.py:373
  106.0 12.6 %collective-permute-start.27 = (bf16[64,2304]{1,0:T(8,128)(2,1)S(1)}, bf16[64,2304]{1,0:T(8,128)(2,1)S(1)}, u32[]{:S(2)}, u32[]{:S(2)}) collective-permute-start(bf16[64,2304]{1,0:T(8,128)(2,1)S(1)} %add_convert_fusion.1), channel_id=1, source_target_pairs={{0,16},{8,24},{16,0},{24,8},{1,17},{9,25},{17,1},{25,9},{2,18},{10... | collective-permute-start | bytes 884744 | tf_op jit(solution)/shard_map/ppermute | solution.py:373
  107.3 7.5 %collective-permute-start.25 = (bf16[256,128]{1,0:T(8,128)(2,1)S(1)}, bf16[256,128]{1,0:T(8,128)(2,1)S(1)}, u32[]{:S(2)}, u32[]{:S(2)}) collective-permute-start(bf16[256,128]{1,0:T(8,128)(2,1)S(1)} %add_convert_fusion.6), channel_id=1, source_target_pairs={{0,4},{1,5},{2,6},{3,7},{4,0},{5,1},{6,2},{7,3},{8,12},{9,13},{10,... | collective-permute-start | bytes 196616 | tf_op jit(solution)/shard_map/ppermute | solution.py:365
  110.7 6.4 %collective-permute-start.24 = (bf16[320,128]{1,0:T(8,128)(2,1)S(1)}, bf16[320,128]{1,0:T(8,128)(2,1)S(1)}, u32[]{:S(2)}, u32[]{:S(2)}) collective-permute-start(bf16[320,128]{1,0:T(8,128)(2,1)S(1)} %add_convert_fusion.4), channel_id=1, source_target_pairs={{0,4},{1,5},{2,6},{3,7},{4,0},{5,1},{6,2},{7,3},{8,12},{9,13},{10,... | collective-permute-start | bytes 245768 | tf_op jit(solution)/shard_map/ppermute | solution.py:365
  117.1 1.4 %collective-permute-start.26 = (bf16[576,128]{1,0:T(8,128)(2,1)S(1)}, bf16[576,128]{1,0:T(8,128)(2,1)S(1)}, u32[]{:S(2)}, u32[]{:S(2)}) collective-permute-start(bf16[576,128]{1,0:T(8,128)(2,1)S(1)} %pad_maximum_fusion.5), channel_id=1, source_target_pairs={{0,1},{1,0},{2,3},{3,2},{4,5},{5,4},{6,7},{7,6},{8,9},{9,8},{10,11... | collective-permute-start | bytes 442376 | tf_op jit(solution)/shard_map/ppermute | solution.py:311
  119.4 7.8 %collective-permute-start.29 = (bf16[192,512]{1,0:T(8,128)(2,1)S(1)}, bf16[192,512]{1,0:T(8,128)(2,1)S(1)}, u32[]{:S(2)}, u32[]{:S(2)}) collective-permute-start(bf16[192,512]{1,0:T(8,128)(2,1)S(1)} %fusion), channel_id=1, source_target_pairs={{0,8},{8,0},{16,24},{24,16},{1,9},{9,1},{17,25},{25,17},{2,10},{10... | collective-permute-start | bytes 589832 | tf_op jit(solution)/shard_map/ppermute | solution.py:380
  120.9 10.9 %collective-permute-start.30 = (bf16[192,512]{1,0:T(8,128)(2,1)S(1)}, bf16[192,512]{1,0:T(8,128)(2,1)S(1)}, u32[]{:S(2)}, u32[]{:S(2)}) collective-permute-start(bf16[192,512]{1,0:T(8,128)(2,1)S(1)} %fusion), channel_id=1, source_target_pairs={{0,16},{8,24},{16,0},{24,8},{1,17},{9,25},{17,1},{25,9},{2,18},{10... | collective-permute-start | bytes 589832 | tf_op jit(solution)/shard_map/ppermute | solution.py:380
  122.3 9.5 %collective-permute-start.31 = (bf16[192,512]{1,0:T(8,128)(2,1)S(1)}, bf16[192,512]{1,0:T(8,128)(2,1)S(1)}, u32[]{:S(2)}, u32[]{:S(2)}) collective-permute-start(bf16[192,512]{1,0:T(8,128)(2,1)S(1)} %fusion), channel_id=1, source_target_pairs={{0,24},{8,16},{16,8},{24,0},{1,25},{9,17},{17,9},{25,1},{2,26},{10... | collective-permute-start | bytes 589832 | tf_op jit(solution)/shard_map/ppermute | solution.py:380
  (11 other events, 125.8 us)
